TPU v7x, 32 devices: a whole 2x2x4 slice. The times are simulated.
32 devices in a mesh: row: 4 (over x, core), col: 8 (over z, y).
Axes of the slice: x: 2, y: 2, z: 4, core: 2. Of those that a mesh axis runs over, the one named last changes fastest.
Arguments:
- luminance: float32 [512, 4096], P('row', 'col'), may hold values from 0 to 1
- level_gain: float32 [5], replicated, may hold values from 0.5 to 2
Outputs:
- tone_mapped: float32 [512, 4096], P('row', 'col')
All inputs are finite; a program needn't handle non-finite values.
Results may differ from a plain program's by a relative error of at most 0.00002.
Values sent between devices are 32-bit elements; how exact they have to be, the bound alone decides.
A program may use at most 64 MiB of HBM per device.

v0:
```python
import jax
import jax.numpy as jnp
from jax import lax
from jax.sharding import PartitionSpec as P

CHANNELS = 16
LEVELS = 6


binomial = (0.0625, 0.25, 0.375, 0.25, 0.0625)
detail_boost = 1.0
base_slope = 0.5
spread_inverse = 1.0 / (2.0 * 0.025 * 0.025)


def with_halo(block, sides, width):
    for axis, dim in sides:
        count = lax.axis_size(axis)
        forward = [(i, i + 1) for i in range(count - 1)]
        forward.append((count - 1, 0))
        backward = [(target, source) for source, target in forward]
        low = lax.ppermute(
            lax.slice_in_dim(block, block.shape[dim] - width, None, axis=dim), axis, forward
        )
        high = lax.ppermute(lax.slice_in_dim(block, 0, width, axis=dim), axis, backward)
        block = jnp.concatenate([low, block, high], axis=dim)
    return block


def remap_tone(values, anchor, switch):
    offset = values - anchor
    return values + switch * (
        (base_slope - 1.0) * offset
        + detail_boost * offset * jnp.exp(-offset * offset * spread_inverse)
    )


def hat_weights(guidance, anchor):
    return jnp.maximum(0.0, 1.0 - jnp.abs(guidance - anchor) * (CHANNELS - 1))


def down_valid(padded):
    out_rows = (padded.shape[-2] - 4) // 2
    blurred = binomial[0] * padded[..., 0 : 2 * out_rows - 1 : 2, :]
    for step in range(1, 5):
        blurred = blurred + binomial[step] * padded[..., step : step + 2 * out_rows - 1 : 2, :]
    out_cols = (padded.shape[-1] - 4) // 2
    result = binomial[0] * blurred[..., 0 : 2 * out_cols - 1 : 2]
    for step in range(1, 5):
        result = result + binomial[step] * blurred[..., step : step + 2 * out_cols - 1 : 2]
    return result


def up_valid(coarse):
    rows_in = coarse.shape[-2]
    even_rows = (
        coarse[..., 0 : rows_in - 2, :]
        + 6.0 * coarse[..., 1 : rows_in - 1, :]
        + coarse[..., 2:rows_in, :]
    ) * 0.125
    odd_rows = (coarse[..., 1 : rows_in - 1, :] + coarse[..., 2:rows_in, :]) * 0.5
    joined = jnp.stack([even_rows, odd_rows], axis=-2)
    joined = joined.reshape(joined.shape[:-3] + (2 * (rows_in - 2), joined.shape[-1]))
    cols_in = joined.shape[-1]
    even_cols = (
        joined[..., 0 : cols_in - 2] + 6.0 * joined[..., 1 : cols_in - 1] + joined[..., 2:cols_in]
    ) * 0.125
    odd_cols = (joined[..., 1 : cols_in - 1] + joined[..., 2:cols_in]) * 0.5
    result = jnp.stack([even_cols, odd_cols], axis=-1)
    return result.reshape(result.shape[:-2] + (2 * (cols_in - 2),))


def trim_edges(values, margin_in, margin_out):
    cut_width = margin_in - margin_out
    if cut_width == 0:
        return values
    return values[
        ..., cut_width : values.shape[-2] - cut_width, cut_width : values.shape[-1] - cut_width
    ]


def channel_start(padded):
    channel_index = jnp.arange(CHANNELS + 1, dtype=jnp.int32)
    anchors = ((channel_index - 1).astype(jnp.float32) / (CHANNELS - 1))[:, None, None]
    switches = (channel_index > 0).astype(jnp.float32)[:, None, None]
    return down_valid(remap_tone(padded[None], anchors, switches))


def rim_levels(channels):
    return with_halo(channels, (("row", 1), ("col", 2)), 2)


def level_term(fine_all, guidance, coarse_channels, coarse_margin, margin_out, gain):
    kept_coarse = (margin_out + 1) // 2 + 1
    anchors = (jnp.arange(CHANNELS, dtype=jnp.int32).astype(jnp.float32) / (CHANNELS - 1))[
        :, None, None
    ]
    widened = up_valid(trim_edges(coarse_channels[1:], coarse_margin, kept_coarse))
    widened = trim_edges(widened, 2 * kept_coarse - 2, margin_out)
    detail = fine_all - widened
    running = jnp.sum(hat_weights(guidance[None], anchors) * detail, axis=0)
    return gain * running


def local(luminance, level_gain):
    padded = with_halo(luminance, (("row", 0), ("col", 1)), 2)
    pyramids = [None]
    margins = [2]
    current = channel_start(padded)
    for level_index in range(1, LEVELS):
        extended = rim_levels(current)
        pyramids.append(extended)
        margins.append(2)
        if level_index < LEVELS - 1:
            current = down_valid(extended)
    kept_margins = [0 for level_index in range(LEVELS)]
    anchors = (jnp.arange(CHANNELS, dtype=jnp.int32).astype(jnp.float32) / (CHANNELS - 1))[
        :, None, None
    ]
    coefficients = []
    for level_index in range(LEVELS - 1):
        margin_out = kept_margins[level_index]
        if level_index == 0:
            guidance = luminance
            fine_all = remap_tone(luminance[None], anchors, 1.0)
        else:
            guidance = trim_edges(pyramids[level_index][0], margins[level_index], margin_out)
            fine_all = trim_edges(pyramids[level_index][1:], margins[level_index], margin_out)
        coefficients.append(
            level_term(
                fine_all,
                guidance,
                pyramids[level_index + 1],
                margins[level_index + 1],
                margin_out,
                level_gain[level_index],
            )
        )
    result = trim_edges(pyramids[LEVELS - 1][0], margins[LEVELS - 1], kept_margins[LEVELS - 1])
    for level_index in reversed(range(LEVELS - 1)):
        widened = up_valid(with_halo(result, (("row", 0), ("col", 1)), 1))
        result = coefficients[level_index] + widened
    return result


def solution(mesh):
    placed = (P("row", "col"), P())
    return jax.shard_map(
        local, mesh=mesh, in_specs=placed, out_specs=P("row", "col"), check_vma=False
    )
```

profile of v0, /device:TPU:0, one launch (start us, length us, event | category | flops | bytes accessed | tf_op | source)
XLA Modules:
  0.0 522.8 jit_solution(11897798258832523415)
XLA Ops:
  17.4 3.4 multiply_add_fusion
  20.8 40.6 %slice.617 = f32[17,64,256]{2,0,1:T(8,128)S(1)} slice(f32[17,64,516]{2,0,1:T(8,128)} %multiply_add_fusion), slice={[0:17:1], [0:64:1], [0:511:2]} | slice | bytes 2228224 | tf_op jit(solution)/shard_map/slice | solution.py:48
  61.4 41.0 %slice.618 = f32[17,64,256]{2,0,1:T(8,128)} slice(f32[17,64,516]{2,0,1:T(8,128)} %multiply_add_fusion), slice={[0:17:1], [0:64:1], [1:512:2]} | slice | bytes 2228224 | tf_op jit(solution)/shard_map/slice | solution.py:50
  102.3 41.0 %slice.619 = f32[17,64,256]{2,0,1:T(8,128)} slice(f32[17,64,516]{2,0,1:T(8,128)} %multiply_add_fusion), slice={[0:17:1], [0:64:1], [2:513:2]} | slice | bytes 2228224 | tf_op jit(solution)/shard_map/slice | solution.py:50
  143.3 41.2 %slice.620 = f32[17,64,256]{2,0,1:T(8,128)} slice(f32[17,64,516]{2,0,1:T(8,128)} %multiply_add_fusion), slice={[0:17:1], [0:64:1], [3:514:2]} | slice | bytes 2228224 | tf_op jit(solution)/shard_map/slice | solution.py:50
  184.5 41.0 %slice.621 = f32[17,64,256]{2,0,1:T(8,128)} slice(f32[17,64,516]{2,0,1:T(8,128)} %multiply_add_fusion), slice={[0:17:1], [0:64:1], [4:515:2]} | slice | bytes 2228224 | tf_op jit(solution)/shard_map/slice | solution.py:50
  225.5 3.4 multiply_add_fusion.1
  236.9 3.3 collective-permute-start.7
  248.3 13.6 %slice.641 = f32[17,32,128]{2,0,1:T(8,128)S(1)} slice(f32[17,32,260]{2,0,1:T(8,128)} %multiply_add_fusion.2), slice={[0:17:1], [0:32:1], [0:255:2]} | slice | bytes 557056 | tf_op jit(solution)/shard_map/slice | solution.py:48
  261.9 13.7 %slice.642 = f32[17,32,128]{2,0,1:T(8,128)} slice(f32[17,32,260]{2,0,1:T(8,128)} %multiply_add_fusion.2), slice={[0:17:1], [0:32:1], [1:256:2]} | slice | bytes 557056 | tf_op jit(solution)/shard_map/slice | solution.py:50
  275.6 13.7 %slice.643 = f32[17,32,128]{2,0,1:T(8,128)} slice(f32[17,32,260]{2,0,1:T(8,128)} %multiply_add_fusion.2), slice={[0:17:1], [0:32:1], [2:257:2]} | slice | bytes 557056 | tf_op jit(solution)/shard_map/slice | solution.py:50
  289.3 13.8 %slice.644 = f32[17,32,128]{2,0,1:T(8,128)} slice(f32[17,32,260]{2,0,1:T(8,128)} %multiply_add_fusion.2), slice={[0:17:1], [0:32:1], [3:258:2]} | slice | bytes 557056 | tf_op jit(solution)/shard_map/slice | solution.py:50
  303.1 13.7 %slice.645 = f32[17,32,128]{2,0,1:T(8,128)} slice(f32[17,32,260]{2,0,1:T(8,128)} %multiply_add_fusion.2), slice={[0:17:1], [0:32:1], [4:259:2]} | slice | bytes 557056 | tf_op jit(solution)/shard_map/slice | solution.py:50
  322.5 4.1 collective-permute-start.11
  328.1 13.9 %collective-permute-done.10 = f32[17,36,2]{2,0,1:T(8,128)S(1)} collective-permute-done((f32[17,36,2]{2,0,1:T(8,128)S(1)}, f32[17,36,2]{2,0,1:T(8,128)S(1)}, u32[]{:S(2)}, u32[]{:S(2)}) %collective-permute-start.10) | collective-permute-done | bytes 4928 | tf_op jit(solution)/shard_map/ppermute | solution.py:22
  347.4 4.1 slice.665
  351.6 4.0 slice.666
  355.6 4.0 slice.667
  359.6 4.0 slice.668
  363.6 4.0 slice.669
  372.5 4.7 collective-permute-start.15
  380.2 3.6 collective-permute-done.14
  405.2 5.0 collective-permute-start.19
  434.4 4.7 collective-permute-start.23
  454.7 4.7 collective-permute-start.27
  468.1 4.8 collective-permute-start.31
  480.7 4.8 collective-permute-start.35
  492.1 4.0 copy.97
  496.2 3.8 copy.98
  500.1 4.8 collective-permute-start.39
  511.6 5.0 collective-permute-start.43
  516.6 3.3 fusion.9
  (270 shorter events, 146.8 us)
Async XLA Ops:
  0.7 3.7 collective-permute-start
  5.5 7.8 %collective-permute-start.2 = (f32[132,2]{1,0:T(8,128)S(1)}, f32[132,2]{1,0:T(8,128)S(1)}, u32[]{:S(2)}, u32[]{:S(2)}) collective-permute-start(f32[132,2]{1,0:T(8,128)S(1)} %get-tuple-element.21), channel_id=1, source_target_pairs={{0,1},{1,2},{2,3},{3,4},{4,5},{5,6},{6,7},{7,0},{8,9},{9,10},{10,1... | collective-permute-start | bytes 3176 | tf_op jit(solution)/shard_map/ppermute | solution.py:22
  7.8 5.7 %collective-permute-start.3 = (f32[132,2]{1,0:T(8,128)S(1)}, f32[132,2]{1,0:T(8,128)S(1)}, u32[]{:S(2)}, u32[]{:S(2)}) collective-permute-start(f32[132,2]{1,0:T(8,128)S(1)} %get-tuple-element.22), channel_id=1, source_target_pairs={{1,0},{2,1},{3,2},{4,3},{5,4},{6,5},{7,6},{0,7},{9,8},{10,9},{11,1... | collective-permute-start | bytes 3176 | tf_op jit(solution)/shard_map/ppermute | solution.py:25
  228.9 3.6 collective-permute-start.4
  235.2 6.5 %collective-permute-start.6 = (f32[17,68,2]{1,2,0:T(2,128)S(1)}, f32[17,68,2]{1,2,0:T(2,128)S(1)}, u32[]{:S(2)}, u32[]{:S(2)}) collective-permute-start(f32[17,68,2]{1,2,0:T(2,128)S(1)} %copy.87), channel_id=1, source_target_pairs={{0,1},{1,2},{2,3},{3,4},{4,5},{5,6},{6,7},{7,0},{8,9},{9,10},{10,1... | collective-permute-start | bytes 27752 | tf_op jit(solution)/shard_map/ppermute | solution.py:22
  236.9 6.0 %collective-permute-start.7 = (f32[17,68,2]{1,2,0:T(2,128)S(1)}, f32[17,68,2]{1,2,0:T(2,128)S(1)}, u32[]{:S(2)}, u32[]{:S(2)}) collective-permute-start(f32[17,68,2]{1,2,0:T(2,128)S(1)} %copy.88), channel_id=1, source_target_pairs={{1,0},{2,1},{3,2},{4,3},{5,4},{6,5},{7,6},{0,7},{9,8},{10,9},{11,1... | collective-permute-start | bytes 27752 | tf_op jit(solution)/shard_map/ppermute | solution.py:25
  318.3 3.3 collective-permute-start.8
  321.8 20.1 %collective-permute-start.10 = (f32[17,36,2]{2,0,1:T(8,128)S(1)}, f32[17,36,2]{2,0,1:T(8,128)S(1)}, u32[]{:S(2)}, u32[]{:S(2)}) collective-permute-start(f32[17,36,2]{2,0,1:T(8,128)S(1)} %get-tuple-element.17), channel_id=1, source_target_pairs={{0,1},{1,2},{2,3},{3,4},{4,5},{5,6},{6,7},{7,0},{8,9},{9,10},{10,1... | collective-permute-start | bytes 14696 | tf_op jit(solution)/shard_map/ppermute | solution.py:22
  322.5 22.2 %collective-permute-start.11 = (f32[17,36,2]{2,0,1:T(8,128)S(1)}, f32[17,36,2]{2,0,1:T(8,128)S(1)}, u32[]{:S(2)}, u32[]{:S(2)}) collective-permute-start(f32[17,36,2]{2,0,1:T(8,128)S(1)} %get-tuple-element.18), channel_id=1, source_target_pairs={{1,0},{2,1},{3,2},{4,3},{5,4},{6,5},{7,6},{0,7},{9,8},{10,9},{11,1... | collective-permute-start | bytes 14696 | tf_op jit(solution)/shard_map/ppermute | solution.py:25
  368.9 3.3 collective-permute-start.12
  372.4 11.4 %collective-permute-start.14 = (f32[17,20,2]{2,0,1:T(8,128)S(1)}, f32[17,20,2]{2,0,1:T(8,128)S(1)}, u32[]{:S(2)}, u32[]{:S(2)}) collective-permute-start(f32[17,20,2]{2,0,1:T(8,128)S(1)} %get-tuple-element.29), channel_id=1, source_target_pairs={{0,1},{1,2},{2,3},{3,4},{4,5},{5,6},{6,7},{7,0},{8,9},{9,10},{10,1... | collective-permute-start | bytes 8168 | tf_op jit(solution)/shard_map/ppermute | solution.py:22
  372.5 13.8 %collective-permute-start.15 = (f32[17,20,2]{2,0,1:T(8,128)S(1)}, f32[17,20,2]{2,0,1:T(8,128)S(1)}, u32[]{:S(2)}, u32[]{:S(2)}) collective-permute-start(f32[17,20,2]{2,0,1:T(8,128)S(1)} %get-tuple-element.30), channel_id=1, source_target_pairs={{1,0},{2,1},{3,2},{4,3},{5,4},{6,5},{7,6},{0,7},{9,8},{10,9},{11,1... | collective-permute-start | bytes 8168 | tf_op jit(solution)/shard_map/ppermute | solution.py:25
  401.1 3.3 collective-permute-start.16
  405.2 12.5 %collective-permute-start.18 = (f32[17,12,2]{2,0,1:T(8,128)}, f32[17,12,2]{2,0,1:T(8,128)}, u32[]{:S(2)}, u32[]{:S(2)}) collective-permute-start(f32[17,12,2]{2,0,1:T(8,128)} %get-tuple-element.37), channel_id=1, source_target_pairs={{0,1},{1,2},{2,3},{3,4},{4,5},{5,6},{6,7},{7,0},{8,9},{9,10},{10,1... | collective-permute-start | bytes 4904 | tf_op jit(solution)/shard_map/ppermute | solution.py:22
  405.2 12.5 %collective-permute-start.19 = (f32[17,12,2]{2,0,1:T(8,128)}, f32[17,12,2]{2,0,1:T(8,128)}, u32[]{:S(2)}, u32[]{:S(2)}) collective-permute-start(f32[17,12,2]{2,0,1:T(8,128)} %get-tuple-element.38), channel_id=1, source_target_pairs={{1,0},{2,1},{3,2},{4,3},{5,4},{6,5},{7,6},{0,7},{9,8},{10,9},{11,1... | collective-permute-start | bytes 4904 | tf_op jit(solution)/shard_map/ppermute | solution.py:25
  434.4 10.4 %collective-permute-start.22 = (f32[17,8,2]{2,0,1:T(8,128)}, f32[17,8,2]{2,0,1:T(8,128)}, u32[]{:S(2)}, u32[]{:S(2)}) collective-permute-start(f32[17,8,2]{2,0,1:T(8,128)} %get-tuple-element.45), channel_id=1, source_target_pairs={{0,1},{1,2},{2,3},{3,4},{4,5},{5,6},{6,7},{7,0},{8,9},{9,10},{10,1... | collective-permute-start | bytes 3272 | tf_op jit(solution)/shard_map/ppermute | solution.py:22
  434.4 10.4 %collective-permute-start.23 = (f32[17,8,2]{2,0,1:T(8,128)}, f32[17,8,2]{2,0,1:T(8,128)}, u32[]{:S(2)}, u32[]{:S(2)}) collective-permute-start(f32[17,8,2]{2,0,1:T(8,128)} %get-tuple-element.46), channel_id=1, source_target_pairs={{1,0},{2,1},{3,2},{4,3},{5,4},{6,5},{7,6},{0,7},{9,8},{10,9},{11,1... | collective-permute-start | bytes 3272 | tf_op jit(solution)/shard_map/ppermute | solution.py:25
  451.2 3.4 collective-permute-start.24
  454.7 6.3 %collective-permute-start.26 = (f32[6,1]{1,0:T(8,128)S(1)}, f32[6,1]{1,0:T(8,128)S(1)}, u32[]{:S(2)}, u32[]{:S(2)}) collective-permute-start(f32[6,1]{1,0:T(8,128)S(1)} %get-tuple-element.85), channel_id=1, source_target_pairs={{0,1},{1,2},{2,3},{3,4},{4,5},{5,6},{6,7},{7,0},{8,9},{9,10},{10,1... | collective-permute-start | bytes 80 | tf_op jit(solution)/shard_map/ppermute | solution.py:22
  454.7 6.3 %collective-permute-start.27 = (f32[6,1]{1,0:T(8,128)S(1)}, f32[6,1]{1,0:T(8,128)S(1)}, u32[]{:S(2)}, u32[]{:S(2)}) collective-permute-start(f32[6,1]{1,0:T(8,128)S(1)} %get-tuple-element.86), channel_id=1, source_target_pairs={{1,0},{2,1},{3,2},{4,3},{5,4},{6,5},{7,6},{0,7},{9,8},{10,9},{11,1... | collective-permute-start | bytes 80 | tf_op jit(solution)/shard_map/ppermute | solution.py:25
  464.6 3.5 collective-permute-start.28
  464.7 3.3 collective-permute-start.29
  468.1 6.3 %collective-permute-start.30 = (f32[10,1]{1,0:T(8,128)S(1)}, f32[10,1]{1,0:T(8,128)S(1)}, u32[]{:S(2)}, u32[]{:S(2)}) collective-permute-start(f32[10,1]{1,0:T(8,128)S(1)} %get-tuple-element.77), channel_id=1, source_target_pairs={{0,1},{1,2},{2,3},{3,4},{4,5},{5,6},{6,7},{7,0},{8,9},{9,10},{10,1... | collective-permute-start | bytes 128 | tf_op jit(solution)/shard_map/ppermute | solution.py:22
  468.1 6.3 %collective-permute-start.31 = (f32[10,1]{1,0:T(8,128)S(1)}, f32[10,1]{1,0:T(8,128)S(1)}, u32[]{:S(2)}, u32[]{:S(2)}) collective-permute-start(f32[10,1]{1,0:T(8,128)S(1)} %get-tuple-element.78), channel_id=1, source_target_pairs={{1,0},{2,1},{3,2},{4,3},{5,4},{6,5},{7,6},{0,7},{9,8},{10,9},{11,1... | collective-permute-start | bytes 128 | tf_op jit(solution)/shard_map/ppermute | solution.py:25
  480.7 6.4 %collective-permute-start.34 = (f32[18,1]{1,0:T(8,128)S(1)}, f32[18,1]{1,0:T(8,128)S(1)}, u32[]{:S(2)}, u32[]{:S(2)}) collective-permute-start(f32[18,1]{1,0:T(8,128)S(1)} %get-tuple-element.69), channel_id=1, source_target_pairs={{0,1},{1,2},{2,3},{3,4},{4,5},{5,6},{6,7},{7,0},{8,9},{9,10},{10,1... | collective-permute-start | bytes 224 | tf_op jit(solution)/shard_map/ppermute | solution.py:22
  480.7 6.4 %collective-permute-start.35 = (f32[18,1]{1,0:T(8,128)S(1)}, f32[18,1]{1,0:T(8,128)S(1)}, u32[]{:S(2)}, u32[]{:S(2)}) collective-permute-start(f32[18,1]{1,0:T(8,128)S(1)} %get-tuple-element.70), channel_id=1, source_target_pairs={{1,0},{2,1},{3,2},{4,3},{5,4},{6,5},{7,6},{0,7},{9,8},{10,9},{11,1... | collective-permute-start | bytes 224 | tf_op jit(solution)/shard_map/ppermute | solution.py:25
  488.1 11.9 %collective-permute-start.36 = (f32[1,128]{1,0:T(1,128)S(1)}, f32[1,128]{1,0:T(1,128)S(1)}, u32[]{:S(2)}, u32[]{:S(2)}) collective-permute-start(f32[1,128]{1,0:T(1,128)S(1)} %get-tuple-element.63), channel_id=1, source_target_pairs={{0,8},{8,16},{16,24},{24,0},{1,9},{9,17},{17,25},{25,1},{2,10},{10... | collective-permute-start | bytes 1544 | tf_op jit(solution)/shard_map/ppermute | solution.py:22
  488.8 11.2 %collective-permute-start.37 = (f32[1,128]{1,0:T(1,128)S(1)}, f32[1,128]{1,0:T(1,128)S(1)}, u32[]{:S(2)}, u32[]{:S(2)}) collective-permute-start(f32[1,128]{1,0:T(1,128)S(1)} %get-tuple-element.64), channel_id=1, source_target_pairs={{8,0},{16,8},{24,16},{0,24},{9,1},{17,9},{25,17},{1,25},{10,2},{18... | collective-permute-start | bytes 1544 | tf_op jit(solution)/shard_map/ppermute | solution.py:25
  500.1 7.1 %collective-permute-start.38 = (f32[34,1]{1,0:T(8,128)S(1)}, f32[34,1]{1,0:T(8,128)S(1)}, u32[]{:S(2)}, u32[]{:S(2)}) collective-permute-start(f32[34,1]{1,0:T(8,128)S(1)} %get-tuple-element.61), channel_id=1, source_target_pairs={{0,1},{1,2},{2,3},{3,4},{4,5},{5,6},{6,7},{7,0},{8,9},{9,10},{10,1... | collective-permute-start | bytes 416 | tf_op jit(solution)/shard_map/ppermute | solution.py:22
  500.1 7.1 %collective-permute-start.39 = (f32[34,1]{1,0:T(8,128)S(1)}, f32[34,1]{1,0:T(8,128)S(1)}, u32[]{:S(2)}, u32[]{:S(2)}) collective-permute-start(f32[34,1]{1,0:T(8,128)S(1)} %get-tuple-element.62), channel_id=1, source_target_pairs={{1,0},{2,1},{3,2},{4,3},{5,4},{6,5},{7,6},{0,7},{9,8},{10,9},{11,1... | collective-permute-start | bytes 416 | tf_op jit(solution)/shard_map/ppermute | solution.py:25
  511.6 8.3 %collective-permute-start.42 = (f32[66,1]{1,0:T(8,128)S(1)}, f32[66,1]{1,0:T(8,128)S(1)}, u32[]{:S(2)}, u32[]{:S(2)}) collective-permute-start(f32[66,1]{1,0:T(8,128)S(1)} %get-tuple-element.49), channel_id=1, source_target_pairs={{0,1},{1,2},{2,3},{3,4},{4,5},{5,6},{6,7},{7,0},{8,9},{9,10},{10,1... | collective-permute-start | bytes 800 | tf_op jit(solution)/shard_map/ppermute | solution.py:22
  511.6 8.3 %collective-permute-start.43 = (f32[66,1]{1,0:T(8,128)S(1)}, f32[66,1]{1,0:T(8,128)S(1)}, u32[]{:S(2)}, u32[]{:S(2)}) collective-permute-start(f32[66,1]{1,0:T(8,128)S(1)} %get-tuple-element.50), channel_id=1, source_target_pairs={{1,0},{2,1},{3,2},{4,3},{5,4},{6,5},{7,6},{0,7},{9,8},{10,9},{11,1... | collective-permute-start | bytes 800 | tf_op jit(solution)/shard_map/ppermute | solution.py:25
  (29 other events, 341.9 us)
where the time goes:
time: 528 us; the launch traced here: 523 us
  local copies, waits for them, and re-layouts  353 us (67%)
  starting transfers between devices  73.8 us (14%)
  other arithmetic  58.1 us (11%)
  waiting for transfers between devices  36.5 us (7%)
    slice x20, local copies, waits for them, and re-layouts, down_valid(): blurred[..., step:step + 2 * out_cols - 1:2]  250 us
    ppermute x22, starting transfers between devices, with_halo(): lax.ppermute(lax.slice_in_dim(block, 0, width, axis=dim), axis, backward)  63.5 us
    slice x5, local copies, waits for them, and re-layouts, down_valid(): result = binomial[0] * blurred[..., 0:2 * out_cols - 1:2]  62.1 us
    ppermute x22, waiting for transfers between devices, with_halo(): lax.ppermute(lax.slice_in_dim(block, block.shape[dim] - width, None, axis...  30.7 us
    another operation x8, local copies, waits for them, and re-layouts, up_valid(): result = jnp.stack([even_cols, odd_cols], axis=-1)  12.3 us
    reshape x8, local copies, waits for them, and re-layouts, up_valid(): return result.reshape(result.shape[:-2] + (2 * (cols_in - 2),))  11.4 us
  transfers between devices with their start and end apart: 44, of which 21 were waited for; matrix products, arithmetic and copies ran while one was open for 9% of the time, Pallas kernels for 0%

commit v1 on v0

v1 whole, which is shorter than its diff:
```python
import functools
import jax
import jax.numpy as jnp
import numpy as np
from jax import lax
from jax.experimental import pallas as pl
from jax.experimental.pallas import tpu as pltpu
from jax.sharding import PartitionSpec as P

CHANNELS = 16
LEVELS = 6
HALO_ROWS = 96
HALO_COLS = 128
PAD = 8
LANE = 128

base_slope = 0.5
spread_inverse = 1.0 / (2.0 * 0.025 * 0.025)
MESH = pl.DeviceIdType.MESH


def sizes(block_rows, block_cols):
    rows = [(block_rows + 2 * HALO_ROWS) >> level for level in range(LEVELS)]
    cols = [(block_cols + 2 * HALO_COLS) >> level for level in range(LEVELS)]
    tiles = [-(-c // LANE) for c in cols]
    return rows, cols, tiles


def down_matrix(cols_in, cols_out, tiles_in, tiles_out):
    matrix = np.zeros((tiles_in * LANE, tiles_out * LANE), np.float32)
    for j in range(cols_out):
        for s, weight in enumerate((0.0625, 0.25, 0.375, 0.25, 0.0625)):
            source = 2 * j + s - 2
            if 0 <= source < cols_in:
                matrix[source, j] = weight
    return matrix


def up_matrix(coarse_cols, first, count, tiles_in, tiles_out):
    matrix = np.zeros((tiles_in * LANE, tiles_out * LANE), np.float32)
    for f in range(count):
        m = first + f // 2
        taps = ((m - 1, 0.125), (m, 0.75), (m + 1, 0.125)) if f % 2 == 0 else ((m, 0.5), (m + 1, 0.5))
        for source, weight in taps:
            if 0 <= source < coarse_cols:
                matrix[source, f] = weight
    return matrix


def exchange_kernel(axes, lum, ext, own_sem, send_sem, recv_sem):
    block_rows, block_cols = lum.shape
    row_axis, col_axis = axes
    row, col = lax.axis_index(row_axis), lax.axis_index(col_axis)
    row_count, col_count = lax.axis_size(row_axis), lax.axis_size(col_axis)
    steps = [(dr, dc) for dr in (-1, 0, 1) for dc in (-1, 0, 1) if (dr, dc) != (0, 0)]

    def device(dr, dc):
        return (lax.rem(row + dr + row_count, row_count), lax.rem(col + dc + col_count, col_count))

    barrier = pltpu.get_barrier_semaphore()
    for dr, dc in steps:
        pl.semaphore_signal(barrier, inc=1, device_id=device(dr, dc), device_id_type=MESH)
    own = pltpu.make_async_copy(
        lum, ext.at[pl.ds(HALO_ROWS, block_rows), pl.ds(HALO_COLS, block_cols)], own_sem
    )
    own.start()
    pl.semaphore_wait(barrier, len(steps))

    def span(step, block, halo):
        if step == 0:
            return pl.ds(0, block), pl.ds(halo, block)
        if step < 0:
            return pl.ds(0, halo), pl.ds(halo + block, halo)
        return pl.ds(block - halo, halo), pl.ds(0, halo)

    copies = []
    for index, (dr, dc) in enumerate(steps):
        src_r, dst_r = span(dr, block_rows, HALO_ROWS)
        src_c, dst_c = span(dc, block_cols, HALO_COLS)
        copy = pltpu.make_async_remote_copy(
            src_ref=lum.at[src_r, src_c],
            dst_ref=ext.at[dst_r, dst_c],
            send_sem=send_sem.at[index],
            recv_sem=recv_sem.at[index],
            device_id=device(dr, dc),
            device_id_type=MESH,
        )
        copy.start()
        copies.append(copy)
    own.wait()
    for copy in copies:
        copy.wait()


def exchange(axes, luminance):
    block_rows, block_cols = luminance.shape
    return pl.pallas_call(
        functools.partial(exchange_kernel, axes),
        out_shape=jax.ShapeDtypeStruct(
            (block_rows + 2 * HALO_ROWS, block_cols + 2 * HALO_COLS), jnp.float32
        ),
        in_specs=[pl.BlockSpec(memory_space=pl.ANY)],
        out_specs=pl.BlockSpec(memory_space=pl.ANY),
        scratch_shapes=[
            pltpu.SemaphoreType.DMA,
            pltpu.SemaphoreType.DMA((8,)),
            pltpu.SemaphoreType.DMA((8,)),
        ],
        compiler_params=pltpu.CompilerParams(collective_id=0, has_side_effects=True),
        name="halo_exchange",
    )(luminance)


def mm(x, matrix):
    high = x.astype(jnp.bfloat16)
    low = (x - high.astype(jnp.float32)).astype(jnp.bfloat16)
    return jnp.dot(high, matrix, preferred_element_type=jnp.float32) + jnp.dot(
        low, matrix, preferred_element_type=jnp.float32
    )


def remap_tone(values, anchor):
    offset = values - anchor
    return values + ((base_slope - 1.0) * offset + offset * jnp.exp(-offset * offset * spread_inverse))


def hat(guidance, anchor):
    return jnp.maximum(0.0, 1.0 - jnp.abs(guidance - anchor) * (CHANNELS - 1))


def wide(parts):
    return parts[0] if len(parts) == 1 else jnp.concatenate(parts, axis=1)


def lane(t):
    return slice(t * LANE, (t + 1) * LANE)


def row_down(ref, t, start, count):
    def tap(s):
        return ref[t, pl.ds(start + s - 2, count, stride=2), :]

    return 0.375 * tap(2) + 0.25 * (tap(1) + tap(3)) + 0.0625 * (tap(0) + tap(4))


def row_up(ref, t, start, count):
    before = ref[t, pl.ds(start - 1, count), :]
    here = ref[t, pl.ds(start, count), :]
    after = ref[t, pl.ds(start + 1, count), :]
    return (before + 6.0 * here + after) * 0.125, (here + after) * 0.5


def tone_kernel(rows, tiles, block_rows, block_cols, *refs):
    gain, anchors, lum = refs[:3]
    down = refs[3:8]
    up = refs[8:13]
    out = refs[13]
    center, remapped, first, total, result = refs[14:19]
    stack = (None,) + refs[19:24]
    joined, widened = refs[24:29], refs[29:34]
    collapsed = (None,) + refs[34:39]
    half = block_rows // 2
    own_tiles = block_cols // LANE
    side = HALO_COLS // LANE
    coarse_at = PAD + HALO_ROWS // 2

    for t in range(own_tiles):
        center[t, :, :] = lum[HALO_ROWS : HALO_ROWS + block_rows, lane(side + t)]
    total[...] = jnp.zeros_like(total)

    def shrink(dst_row):
        x = wide([row_down(remapped, t, PAD, rows[1]) for t in range(tiles[0])])
        y = mm(x, down[0][...])
        for t in range(tiles[1]):
            stack[1][t, pl.ds(dst_row, rows[1]), :] = y[:, lane(t)]
        return y

    def channel(k, carry):
        anchor = anchors[k]
        for t in range(tiles[0]):
            for r in range(0, rows[0], 64):
                remapped[t, PAD + r : PAD + r + 64, :] = remap_tone(lum[r : r + 64, lane(t)], anchor)
        y = shrink(pl.multiple_of(PAD + k * rows[1], 8))
        for t in range(tiles[1]):
            first[t, PAD : PAD + rows[1], :] = y[:, lane(t)]
        pairs = [row_up(first, t, coarse_at, half) for t in range(tiles[1])]
        x = jnp.concatenate([wide([p[0] for p in pairs]), wide([p[1] for p in pairs])], axis=0)
        fine = mm(x, up[0][...])
        for t in range(own_tiles):
            for p in range(2):
                guidance = center[t, pl.ds(p, half, stride=2), :]
                value = remapped[side + t, pl.ds(PAD + HALO_ROWS + p, half, stride=2), :]
                total[t, p * half : (p + 1) * half, :] += hat(guidance, anchor) * (
                    value - fine[p * half : (p + 1) * half, lane(t)]
                )
        return carry

    lax.fori_loop(0, CHANNELS, channel, 0)
    for t in range(tiles[0]):
        for r in range(0, rows[0], 64):
            remapped[t, PAD + r : PAD + r + 64, :] = lum[r : r + 64, lane(t)]
    shrink(PAD + CHANNELS * rows[1])

    for level in range(1, LEVELS - 1):
        count = (CHANNELS + 1) * rows[level + 1]
        chunk = count // 5 if count % 40 == 0 else count
        for o in range(0, count, chunk):
            x = wide([row_down(stack[level], t, PAD + 2 * o, chunk) for t in range(tiles[level])])
            y = mm(x, down[level][...])
            for t in range(tiles[level + 1]):
                stack[level + 1][t, PAD + o : PAD + o + chunk, :] = y[:, lane(t)]

    coefficients = [None] * LEVELS
    low = [0, 40, 0, 0, 0]
    high = [0, 120] + rows[2:5]
    for level in range(1, LEVELS - 1):
        fine, coarse = rows[level], rows[level + 1]
        chunk = coarse if coarse % 8 == 0 else CHANNELS * coarse
        spread, wider = joined[level], widened[level]
        for o in range(0, CHANNELS * coarse, chunk):
            for t in range(tiles[level + 1]):
                even, odd = row_up(stack[level + 1], t, PAD + o, chunk)
                spread[t, pl.ds(2 * o, chunk, stride=2), :] = even
                spread[t, pl.ds(2 * o + 1, chunk, stride=2), :] = odd
            x = wide([spread[t, 2 * o : 2 * (o + chunk), :] for t in range(tiles[level + 1])])
            y = mm(x, up[level][...])
            for t in range(tiles[level]):
                wider[t, 2 * o : 2 * (o + chunk), :] = y[:, lane(t)]
        a, b = low[level], high[level]
        sums = []
        for t in range(tiles[level]):
            guidance = stack[level][t, PAD + CHANNELS * fine + a : PAD + CHANNELS * fine + b, :]
            running = None
            for k in range(CHANNELS):
                anchor = np.float32(k) / np.float32(CHANNELS - 1)
                term = hat(guidance, anchor) * (
                    stack[level][t, PAD + k * fine + a : PAD + k * fine + b, :]
                    - wider[t, k * fine + a : k * fine + b, :]
                )
                running = term if running is None else running + term
            sums.append(gain[level] * running)
        coefficients[level] = sums

    last = LEVELS - 1
    guide_at = PAD + CHANNELS * rows[last]
    for t in range(tiles[last]):
        collapsed[last][t, PAD : PAD + rows[last], :] = stack[last][t, guide_at : guide_at + rows[last], :]
    for level in range(LEVELS - 2, 0, -1):
        a, b = low[level], high[level]
        for t in range(tiles[level + 1]):
            even, odd = row_up(collapsed[level + 1], t, PAD + a // 2, (b - a) // 2)
            joined[0][t, pl.ds(0, (b - a) // 2, stride=2), :] = even
            joined[0][t, pl.ds(1, (b - a) // 2, stride=2), :] = odd
        x = wide([joined[0][t, 0 : b - a, :] for t in range(tiles[level + 1])])
        y = mm(x, up[level][...])
        for t in range(tiles[level]):
            collapsed[level][t, PAD + a : PAD + b, :] = coefficients[level][t] + y[:, lane(t)]
    pairs = [row_up(collapsed[1], t, coarse_at, half) for t in range(tiles[1])]
    x = jnp.concatenate([wide([p[0] for p in pairs]), wide([p[1] for p in pairs])], axis=0)
    fine = mm(x, up[0][...])
    for t in range(own_tiles):
        for p in range(2):
            result[t, pl.ds(p, half, stride=2), :] = (
                gain[0] * total[t, p * half : (p + 1) * half, :]
                + fine[p * half : (p + 1) * half, lane(t)]
            )
        out[:, lane(t)] = result[t, :, :]


def tone(extended, level_gain, block_rows, block_cols):
    rows, cols, tiles = sizes(block_rows, block_cols)
    anchors = np.arange(CHANNELS, dtype=np.float32) / np.float32(CHANNELS - 1)
    down = [
        down_matrix(cols[l], cols[l + 1], tiles[l], tiles[l + 1]) for l in range(LEVELS - 1)
    ]
    up = [up_matrix(cols[1], HALO_COLS // 2, block_cols, tiles[1], block_cols // LANE)] + [
        up_matrix(cols[l + 1], 0, cols[l], tiles[l + 1], tiles[l]) for l in range(1, LEVELS - 1)
    ]

    def f32(*shape):
        return pltpu.VMEM(shape, jnp.float32)

    def padded(count):
        return -(-count // 8) * 8 + 2 * PAD

    scratch = [
        f32(block_cols // LANE, block_rows, LANE),
        f32(tiles[0], rows[0] + 2 * PAD, LANE),
        f32(tiles[1], rows[1] + 2 * PAD, LANE),
        f32(block_cols // LANE, block_rows, LANE),
        f32(block_cols // LANE, block_rows, LANE),
    ]
    scratch += [f32(tiles[l], padded((CHANNELS + 1) * rows[l]), LANE) for l in range(1, LEVELS)]
    scratch += [f32(tiles[1], padded(rows[1]), LANE)]
    scratch += [f32(tiles[l + 1], padded(CHANNELS * rows[l]), LANE) for l in range(1, LEVELS - 1)]
    scratch += [f32(1, 8, LANE)]
    scratch += [f32(tiles[l], padded(CHANNELS * rows[l]), LANE) for l in range(1, LEVELS - 1)]
    scratch += [f32(tiles[l], padded(rows[l]), LANE) for l in range(1, LEVELS)]
    vmem = pl.BlockSpec(memory_space=pltpu.VMEM)
    smem = pl.BlockSpec(memory_space=pltpu.SMEM)
    return pl.pallas_call(
        functools.partial(tone_kernel, rows, tiles, block_rows, block_cols),
        out_shape=jax.ShapeDtypeStruct((block_rows, block_cols), jnp.float32),
        in_specs=[smem, smem] + [vmem] * 11,
        out_specs=vmem,
        scratch_shapes=scratch,
        compiler_params=pltpu.CompilerParams(vmem_limit_bytes=48 * 1024 * 1024),
        name="tone_pyramid",
    )(level_gain, jnp.asarray(anchors), extended, *[jnp.asarray(m, jnp.bfloat16) for m in down + up])


def solution(mesh):
    placed = (P("row", "col"), P())

    def local(luminance, level_gain):
        extended = exchange(("row", "col"), luminance)
        return tone(extended, level_gain, *luminance.shape)

    return jax.shard_map(
        local, mesh=mesh, in_specs=placed, out_specs=P("row", "col"), check_vma=False
    )
```

time: 528 us -> 47.8 us (0.09)
  local copies, waits for them, and re-layouts: 353 us -> 7.31 us
  starting transfers between devices: 73.8 us -> 0 us
  other arithmetic: 58.1 us -> 0 us
  Pallas kernels: 0 us -> 39.9 us
  waiting for transfers between devices: 36.5 us -> 0 us
    slice x58 -> x0, local copies, waits for them, and re-layouts: 324 us -> none  [the longest x20 250 us: down_valid(): blurred[..., step:step + 2 * out_cols - 1:2]]
    ppermute x44 -> x0, starting transfers between devices: 73.8 us -> none  [the longest x22 63.5 us: with_halo(): lax.ppermute(lax.slice_in_dim(block, 0, width, axis=dim), axis, backward)]
    pallas_call x0 -> x2, Pallas kernels: none -> 39.9 us  [the longest x1 26.1 us: tone(): pl.pallas_call(functools.partial(tone_kernel, rows, tiles, block_rows, bl...]
    ppermute x44 -> x0, waiting for transfers between devices: 36.5 us -> none  [the longest x22 30.7 us: with_halo(): lax.ppermute(lax.slice_in_dim(block, block.shape[dim] - width, None, axis...]
    add x16 -> x0, other arithmetic: 22.2 us -> none  [the longest x5 8.19 us: down_valid(): result + binomial[step] * blurred[..., step:step + 2 * out_cols - 1:2]]
    another operation x38 -> x0, other arithmetic: 16.5 us -> none  [the longest x18 8.48 us: up_valid(): result = jnp.stack([even_cols, odd_cols], axis=-1)]
    another operation x17 -> x0, local copies, waits for them, and re-layouts: 13.1 us -> none  [the longest x8 12.3 us: up_valid(): result = jnp.stack([even_cols, odd_cols], axis=-1)]
    reshape x10 -> x0, local copies, waits for them, and re-layouts: 11.5 us -> none  [the longest x8 11.4 us: up_valid(): return result.reshape(result.shape[:-2] + (2 * (cols_in - 2),))]
  transfers between devices with their start and end apart: 44 -> 0, of which waited for: 21 -> 0; matrix products, arithmetic and copies ran while one was open for 9% -> 0% of each run, Pallas kernels for 0% -> 0%
where the time goes in v1:
time: 47.8 us; the launch traced here: 47.3 us
  Pallas kernels  39.9 us (83%)
  local copies, waits for them, and re-layouts  7.31 us (15%)
    pallas_call x1, Pallas kernels, tone(): pl.pallas_call(functools.partial(tone_kernel, rows, tiles, block_rows, bl...  26.1 us
    pallas_call x1, Pallas kernels, exchange(): pl.pallas_call(functools.partial(exchange_kernel, axes), out_shape=jax.Sh...  13.9 us
    unnamed x26, local copies, waits for them, and re-layouts  7.31 us

profile of v1, /device:TPU:0, one launch (start us, length us, event | category | flops | bytes accessed | tf_op | source)
XLA Modules:
  0.0 47.3 jit_solution(14061467738224913897)
XLA Ops:
  0.0 0.0 copy-start.1
  0.0 0.0 copy-start.2
  0.0 0.0 copy-start.3
  0.0 0.0 copy-start.5
  0.0 13.9 %halo_exchange.1.refs_2_ = f32[320,768]{1,0:T(8,128)} custom-call(f32[128,512]{1,0:T(8,128)} %lum.1), custom_call_target="tpu_custom_call" | custom-call | tf_op jit(solution)/shard_map/halo_exchange/pallas_call | solution.py:97
  13.9 0.0 copy-done.1
  13.9 0.0 copy-done.2
  13.9 0.0 copy-done.3
  13.9 0.0 copy-done.5
  13.9 0.0 copy-start
  13.9 1.2 %copy-done = f32[320,768]{1,0:T(8,128)S(1)} copy-done((f32[320,768]{1,0:T(8,128)S(1)}, f32[320,768]{1,0:T(8,128)}, u32[]{:S(2)}) %copy-start) | copy-done | bytes 983064
  15.1 0.0 copy-start.4
  15.1 0.9 %copy-done.4 = bf16[384,256]{1,0:T(8,128)(2,1)S(1)} copy-done((bf16[384,256]{1,0:T(8,128)(2,1)S(1)}, bf16[384,256]{1,0:T(8,128)(2,1)}, u32[]{:S(2)}) %copy-start.4) | copy-done | bytes 196632
  16.0 0.0 copy-start.6
  16.0 0.8 %copy-done.6 = bf16[256,128]{1,0:T(8,128)(2,1)S(1)} copy-done((bf16[256,128]{1,0:T(8,128)(2,1)S(1)}, bf16[256,128]{1,0:T(8,128)(2,1)}, u32[]{:S(2)}) %copy-start.6) | copy-done | bytes 65560
  16.9 0.0 copy-start.7
  16.9 0.8 %copy-done.7 = bf16[128,128]{1,0:T(8,128)(2,1)S(1)} copy-done((bf16[128,128]{1,0:T(8,128)(2,1)S(1)}, bf16[128,128]{1,0:T(8,128)(2,1)}, u32[]{:S(2)}) %copy-start.7) | copy-done | bytes 32792
  17.6 0.0 copy-start.8
  17.6 0.8 %copy-done.8 = bf16[128,128]{1,0:T(8,128)(2,1)S(1)} copy-done((bf16[128,128]{1,0:T(8,128)(2,1)S(1)}, bf16[128,128]{1,0:T(8,128)(2,1)}, u32[]{:S(2)}) %copy-start.8) | copy-done | bytes 32792
  18.4 0.0 copy-start.9
  18.4 0.8 %copy-done.9 = bf16[128,128]{1,0:T(8,128)(2,1)S(1)} copy-done((bf16[128,128]{1,0:T(8,128)(2,1)S(1)}, bf16[128,128]{1,0:T(8,128)(2,1)}, u32[]{:S(2)}) %copy-start.9) | copy-done | bytes 32792
  19.2 0.0 copy-start.10
  19.2 0.8 %copy-done.10 = bf16[128,128]{1,0:T(8,128)(2,1)S(1)} copy-done((bf16[128,128]{1,0:T(8,128)(2,1)S(1)}, bf16[128,128]{1,0:T(8,128)(2,1)}, u32[]{:S(2)}) %copy-start.10) | copy-done | bytes 32792
  19.9 0.0 copy-start.11
  19.9 0.7 %copy-done.11 = f32[5]{0:T(128)S(1)} copy-done((f32[5]{0:T(128)S(1)}, f32[5]{0:T(128)}, u32[]{:S(2)}) %copy-start.11) | copy-done | bytes 44
  20.6 0.0 copy-start.12
  20.6 0.7 %copy-done.12 = f32[16]{0:T(128)S(1)} copy-done((f32[16]{0:T(128)S(1)}, f32[16]{0:T(128)}, u32[]{:S(2)}) %copy-start.12) | copy-done | bytes 88
  21.2 26.1 %tone_pyramid.1 = f32[128,512]{1,0:T(8,128)} custom-call(f32[5]{0:T(128)S(1)} %copy-done.11, f32[16]{0:T(128)S(1)} %copy-done.12, f32[320,768]{1,0:T(8,128)S(1)} %copy-done, bf16[768,384]{1,0:T(8,128)(2,1)S(1)} %copy-done.1, bf16[384,256]{1,0:T(8,128)(2,1)S(1)} %copy-done.4, bf16[256,128]{1,0:T(8,128)(2,1)S(1)} %copy-done.6, ...), custom_call_target="tpu_custom_call" | custom-call | tf_op jit(solution)/shard_map/tone_pyramid/pallas_call | solution.py:301
Async XLA Ops:
  0.0 13.9 %copy-start.1 = (bf16[768,384]{1,0:T(8,128)(2,1)S(1)}, bf16[768,384]{1,0:T(8,128)(2,1)}, u32[]{:S(2)}) copy-start(bf16[768,384]{1,0:T(8,128)(2,1)} %constant.23.clone.refs_3_) | copy-start | bytes 1769476
  0.0 13.9 %copy-start.2 = (bf16[384,512]{1,0:T(8,128)(2,1)S(1)}, bf16[384,512]{1,0:T(8,128)(2,1)}, u32[]{:S(2)}) copy-start(bf16[384,512]{1,0:T(8,128)(2,1)} %constant.28.clone.refs_8_) | copy-start | bytes 1179652
  0.0 13.9 %copy-start.3 = (bf16[256,384]{1,0:T(8,128)(2,1)S(1)}, bf16[256,384]{1,0:T(8,128)(2,1)}, u32[]{:S(2)}) copy-start(bf16[256,384]{1,0:T(8,128)(2,1)} %constant.29.clone.refs_9_) | copy-start | bytes 589828
  0.0 13.9 %copy-start.5 = (bf16[128,256]{1,0:T(8,128)(2,1)S(1)}, bf16[128,256]{1,0:T(8,128)(2,1)}, u32[]{:S(2)}) copy-start(bf16[128,256]{1,0:T(8,128)(2,1)} %constant.30.clone.refs_10_) | copy-start | bytes 196612
  13.9 1.2 %copy-start = (f32[320,768]{1,0:T(8,128)S(1)}, f32[320,768]{1,0:T(8,128)}, u32[]{:S(2)}) copy-start(f32[320,768]{1,0:T(8,128)} %halo_exchange.1.refs_2_) | copy-start | bytes 2949124
  15.1 0.9 %copy-start.4 = (bf16[384,256]{1,0:T(8,128)(2,1)S(1)}, bf16[384,256]{1,0:T(8,128)(2,1)}, u32[]{:S(2)}) copy-start(bf16[384,256]{1,0:T(8,128)(2,1)} %constant.24.clone.refs_4_) | copy-start | bytes 589828
  16.0 0.8 %copy-start.6 = (bf16[256,128]{1,0:T(8,128)(2,1)S(1)}, bf16[256,128]{1,0:T(8,128)(2,1)}, u32[]{:S(2)}) copy-start(bf16[256,128]{1,0:T(8,128)(2,1)} %constant.25.clone.refs_5_) | copy-start | bytes 196612
  16.9 0.8 %copy-start.7 = (bf16[128,128]{1,0:T(8,128)(2,1)S(1)}, bf16[128,128]{1,0:T(8,128)(2,1)}, u32[]{:S(2)}) copy-start(bf16[128,128]{1,0:T(8,128)(2,1)} %constant.32.clone.refs_12_) | copy-start | bytes 98308
  17.6 0.8 %copy-start.8 = (bf16[128,128]{1,0:T(8,128)(2,1)S(1)}, bf16[128,128]{1,0:T(8,128)(2,1)}, u32[]{:S(2)}) copy-start(bf16[128,128]{1,0:T(8,128)(2,1)} %constant.31.clone.refs_11_) | copy-start | bytes 98308
  18.4 0.8 %copy-start.9 = (bf16[128,128]{1,0:T(8,128)(2,1)S(1)}, bf16[128,128]{1,0:T(8,128)(2,1)}, u32[]{:S(2)}) copy-start(bf16[128,128]{1,0:T(8,128)(2,1)} %constant.27.clone.refs_7_) | copy-start | bytes 98308
  19.2 0.8 %copy-start.10 = (bf16[128,128]{1,0:T(8,128)(2,1)S(1)}, bf16[128,128]{1,0:T(8,128)(2,1)}, u32[]{:S(2)}) copy-start(bf16[128,128]{1,0:T(8,128)(2,1)} %constant.26.clone.refs_6_) | copy-start | bytes 98308
  19.9 0.7 %copy-start.11 = (f32[5]{0:T(128)S(1)}, f32[5]{0:T(128)}, u32[]{:S(2)}) copy-start(f32[5]{0:T(128)} %refs_0_.1) | copy-start | bytes 64
  20.6 0.7 %copy-start.12 = (f32[16]{0:T(128)S(1)}, f32[16]{0:T(128)}, u32[]{:S(2)}) copy-start(f32[16]{0:T(128)} %constant.22.clone.refs_1_) | copy-start | bytes 196

commit v2 on v0

v2 whole, which is shorter than its diff:
```python
import functools
import jax
import jax.numpy as jnp
import numpy as np
from jax import lax
from jax.experimental import pallas as pl
from jax.experimental.pallas import tpu as pltpu
from jax.sharding import PartitionSpec as P

CHANNELS = 16
STACK = CHANNELS + 1
HALO = 32
PAD = 8
LANE = 128
QUARTER = LANE // 4

exponent_scale = -np.log2(np.e) / (2.0 * 0.025 * 0.025)
MESH = pl.DeviceIdType.MESH
STEPS = [(dr, dc) for dr in (-1, 0, 1) for dc in (-1, 0, 1) if (dr, dc) != (0, 0)]


def ceil_to(count, unit):
    return -(-count // unit) * unit


def down_matrix(cols_in, wrap):
    matrix = np.zeros((ceil_to(cols_in, LANE), ceil_to(cols_in // 2, LANE)), np.float32)
    for j in range(cols_in // 2):
        for s, weight in enumerate((0.0625, 0.25, 0.375, 0.25, 0.0625)):
            source = 2 * j + s - 2
            if wrap:
                source %= cols_in
            if 0 <= source < cols_in:
                matrix[source, j] = weight
    return matrix


def up_matrix(fine, place):
    taps = []
    for lane_out, f in enumerate(fine):
        m = f // 2
        weights = ((m - 1, 0.125), (m, 0.75), (m + 1, 0.125)) if f % 2 == 0 else ((m, 0.5), (m + 1, 0.5))
        taps += [(place(source), lane_out, weight) for source, weight in weights]
    taps = [tap for tap in taps if tap[0] is not None]
    matrix = np.zeros((ceil_to(max(t[0] for t in taps) + 1, LANE), ceil_to(len(fine), LANE)), np.float32)
    for source, lane_out, weight in taps:
        matrix[source, lane_out] = weight
    return matrix


def circle(block, level):
    own, side = block >> level, (LANE // 2) >> level
    return list(range(own + side)) + list(range(-side, 0))


def matrices(block_cols):
    def around(level):
        where = {c: i for i, c in enumerate(circle(block_cols, level))}
        return where.get

    def linear(first, count):
        return lambda c: c - first if 0 <= c - first < count else None

    own4 = block_cols >> 4
    down = [down_matrix(len(circle(block_cols, l)), True) for l in range(4)] + [down_matrix(3 * own4, False)]
    up = [up_matrix(list(range(block_cols)), around(1))]
    up += [up_matrix(circle(block_cols, l), around(l + 1)) for l in (1, 2)]
    up += [up_matrix(circle(block_cols, 3), linear(-own4, 3 * own4))]
    up += [up_matrix(list(range(-own4, 2 * own4)), linear(-own4 // 2, 3 * own4 // 2))]
    return down, up


def mm(x, matrix, parts=2):
    total = None
    for part in range(parts):
        head = x.astype(jnp.bfloat16)
        if part < parts - 1:
            x = x - head.astype(jnp.float32)
        term = jnp.dot(head, matrix, preferred_element_type=jnp.float32)
        total = term if total is None else total + term
    return total


def bump(values, anchor):
    offset = values - anchor
    return offset * jnp.exp2(offset * offset * exponent_scale)


def hat(guidance, anchor):
    return jnp.maximum(0.0, 1.0 - jnp.abs(guidance - anchor) * (CHANNELS - 1))


def wide(parts):
    return parts[0] if len(parts) == 1 else jnp.concatenate(parts, axis=1)


def lane(t):
    return slice(t * LANE, (t + 1) * LANE)


def row_down(ref, t, start, count):
    def tap(s):
        return ref[t, pl.ds(start + s - 2, count, stride=2), :]

    return 0.375 * tap(2) + 0.25 * (tap(1) + tap(3)) + 0.0625 * (tap(0) + tap(4))


def row_up(ref, t, start, count):
    before = ref[t, pl.ds(start - 1, count), :]
    here = ref[t, pl.ds(start, count), :]
    after = ref[t, pl.ds(start + 1, count), :]
    return (before + 6.0 * here + after) * 0.125, (here + after) * 0.5


def turn(x, shift):
    shift %= LANE
    return x if shift == 0 else pltpu.roll(x, shift, 1)


def lanes_of(x):
    return lax.broadcasted_iota(jnp.int32, x.shape, 1)


def pack(x, first):
    count = x.shape[0] // 4
    groups = [turn(x[g * count : (g + 1) * count, :], g * QUARTER - first) for g in range(4)]
    return beside(groups)


def beside(groups):
    result = groups[-1]
    index = lanes_of(result)
    for g in reversed(range(len(groups) - 1)):
        result = jnp.where(index < (g + 1) * QUARTER, groups[g], result)
    return result


def chunk_of(count):
    for size in range(320, 0, -8):
        if count % size == 0:
            return size
    return count


def kernel(axes, spans, gain, anchors, lum, bank, out, *refs):
    (top, bottom, side_out, side_in, halo, center, remapped, first, total, result, mats) = refs[:11]
    (g1, g2, g3, g4, e4, g5, u1, u2, u3, u4, v1, v2, v3, v4, c1, c2, c3, c4, c5, packed, gathered) = refs[11:32]
    send_a, recv_a, send_b, recv_b, bank_sem = refs[32:]
    block_rows, block_cols = lum.shape
    own_tiles = block_cols // LANE
    half = block_rows // 2
    counts = [lax.axis_size(a) for a in axes]
    place = [lax.axis_index(a) for a in axes]

    def device(dr, dc):
        return tuple(lax.rem(p + d + n, n) for p, d, n in zip(place, (dr, dc), counts))

    def matrix(name):
        start, depth, width = spans[name]
        return mats[start : start + depth, 0:width]

    bank_copy = pltpu.make_async_copy(bank, mats, bank_sem)
    bank_copy.start()
    barrier = pltpu.get_barrier_semaphore()
    for dr, dc in STEPS:
        pl.semaphore_signal(barrier, inc=1, device_id=device(dr, dc), device_id_type=MESH)

    mid, corner = block_rows // 4, HALO // 4
    for s, (t, start) in enumerate(((0, 0), (own_tiles - 1, LANE - QUARTER))):
        side_out[s, 0:mid, :] = pack(lum[:, lane(t)], start)
        side_out[s, mid : mid + corner, :] = pack(lum[0:HALO, lane(t)], start)
        side_out[s, mid + corner : mid + 2 * corner, :] = pack(lum[block_rows - HALO :, lane(t)], start)
    for t in range(own_tiles):
        center[t, :, :] = lum[:, lane(t)]
    total[...] = jnp.zeros_like(total)
    pl.semaphore_wait(barrier, len(STEPS))

    rows_at = {0: (0, mid), -1: (mid, corner), 1: (mid + corner, corner)}
    copies = []
    for index, (dr, dc) in enumerate(STEPS):
        if dc == 0:
            src = lum.at[pl.ds(0 if dr < 0 else block_rows - HALO, HALO), :]
            dst = bottom if dr < 0 else top
        else:
            s = 0 if dc < 0 else 1
            src = side_out.at[s, pl.ds(*rows_at[dr]), :]
            dst = side_in.at[1 - s, pl.ds(*rows_at[-dr]), :]
        copy = pltpu.make_async_remote_copy(
            src_ref=src,
            dst_ref=dst,
            send_sem=send_a.at[index],
            recv_sem=recv_a.at[index],
            device_id=device(dr, dc),
            device_id_type=MESH,
        )
        copy.start()
        copies.append(copy)
    for copy in copies:
        copy.wait()
    bank_copy.wait()

    ext_rows = block_rows + 2 * HALO
    for start, (at, count) in ((0, rows_at[-1]), (HALO, rows_at[0]), (HALO + block_rows, rows_at[1])):
        left, right = side_in[0, at : at + count, :], side_in[1, at : at + count, :]
        index = lanes_of(left)
        for g in range(4):
            halo[start + g * count : start + (g + 1) * count, :] = jnp.where(
                index < LANE // 2, turn(right, -g * QUARTER), turn(left, LANE - QUARTER - g * QUARTER)
            )

    def extended(t):
        if t == own_tiles:
            return [(r, halo[r : r + 64, :]) for r in range(0, ext_rows, 64)]
        inner = [(HALO + r, lum[r : r + 64, lane(t)]) for r in range(0, block_rows, 64)]
        return [(0, top[:, lane(t)])] + inner + [(HALO + block_rows, bottom[:, lane(t)])]

    rows1 = ext_rows // 2
    tiles1 = first.shape[0]
    coarse_at = PAD + HALO // 2

    def finest(dst_row, prepare, weigh):
        for t in range(own_tiles + 1):
            for r, values in extended(t):
                remapped[t, PAD + r : PAD + r + values.shape[0], :] = prepare(values)
        x = wide([row_down(remapped, t, PAD, rows1) for t in range(own_tiles + 1)])
        y = mm(x, matrix("d0"))
        for t in range(tiles1):
            g1[t, pl.ds(dst_row, rows1), :] = y[:, lane(t)]
            first[t, PAD : PAD + rows1, :] = y[:, lane(t)]
        pairs = [row_up(first, t, coarse_at, half) for t in range(tiles1)]
        x = jnp.concatenate([wide([p[0] for p in pairs]), wide([p[1] for p in pairs])], axis=0)
        fine = mm(x, matrix("u0"))
        for t in range(own_tiles):
            for p in range(2):
                value = remapped[t, pl.ds(PAD + HALO + p, half, stride=2), :]
                total[t, p * half : (p + 1) * half, :] += weigh(t, p) * (
                    value - fine[p * half : (p + 1) * half, lane(t)]
                )

    def channel(k, carry):
        anchor = anchors[k]
        finest(
            pl.multiple_of(PAD + k * rows1, 8),
            lambda values: bump(values, anchor),
            lambda t, p: hat(center[t, pl.ds(p, half, stride=2), :], anchor),
        )
        return carry

    lax.fori_loop(0, CHANNELS, channel, 0)
    finest(PAD + CHANNELS * rows1, lambda values: values, lambda t, p: 0.5)

    def shrink(src, dst, name, count):
        step = chunk_of(count)
        for o in range(0, count, step):
            x = wide([row_down(src, t, PAD + 2 * o, step) for t in range(src.shape[0])])
            y = mm(x, matrix(name))
            for t in range(dst.shape[0]):
                dst[t, PAD + o : PAD + o + step, :] = y[:, lane(t)]

    rows2, rows3, rows4 = rows1 // 2, rows1 // 4, rows1 // 8
    shrink(g1, g2, "d1", STACK * rows2)
    shrink(g2, g3, "d2", STACK * rows3)
    shrink(g3, g4, "d3", STACK * rows4)

    own4 = block_rows // 16
    skip4 = HALO // 16
    groups = -(-STACK // 4)
    for g in range(groups):
        members = []
        for q in range(4):
            k = min(4 * g + q, CHANNELS)
            at = PAD + k * rows4 + skip4
            members.append(turn(g4[0, at : at + own4, :], q * QUARTER))
        packed[g * own4 : (g + 1) * own4, :] = beside(members)
    copies = []
    for index, (dr, dc) in enumerate(STEPS):
        copy = pltpu.make_async_remote_copy(
            src_ref=packed,
            dst_ref=gathered.at[len(STEPS) - 1 - index],
            send_sem=send_b.at[index],
            recv_sem=recv_b.at[index],
            device_id=device(dr, dc),
            device_id_type=MESH,
        )
        copy.start()
        copies.append(copy)

    def detail(level, fine_stack, coarse_stack, spread, wider, name, fine, coarse, skip, a, b):
        count = STACK * coarse
        step = chunk_of(count)
        for o in range(0, count, step):
            for t in range(coarse_stack.shape[0]):
                even, odd = row_up(coarse_stack, t, PAD + o, step)
                spread[t, pl.ds(2 * o, step, stride=2), :] = even
                spread[t, pl.ds(2 * o + 1, step, stride=2), :] = odd
            x = wide([spread[t, 2 * o : 2 * (o + step), :] for t in range(coarse_stack.shape[0])])
            y = mm(x, matrix(name))
            for t in range(fine_stack.shape[0]):
                wider[t, 2 * o : 2 * (o + step), :] = y[:, lane(t)]
        sums = []
        for t in range(fine_stack.shape[0]):

            def difference(k):
                at = k * 2 * coarse + skip
                return (
                    fine_stack[t, PAD + k * fine + a : PAD + k * fine + b, :]
                    - wider[t, at + a : at + b, :]
                )

            guidance = fine_stack[t, PAD + CHANNELS * fine + a : PAD + CHANNELS * fine + b, :]
            running = 0.5 * difference(CHANNELS)
            for k in range(CHANNELS):
                anchor = np.float32(k) / np.float32(CHANNELS - 1)
                running = running + hat(guidance, anchor) * difference(k)
            sums.append(gain[level] * running)
        return sums

    near = HALO // 2 - 8
    coef1 = detail(1, g1, g2, u1, v1, "u1", rows1, rows2, 0, near, rows1 - near)
    coef2 = detail(2, g2, g3, u2, v2, "u2", rows2, rows3, 0, 0, rows2)

    for copy in copies:
        copy.wait()
    for k in range(STACK):
        g, q = divmod(k, 4)
        for dr in (-1, 0, 1):
            members = []
            for dc in (-1, 0, 1):
                if (dr, dc) == (0, 0):
                    piece = packed[g * own4 : (g + 1) * own4, :]
                else:
                    piece = gathered[STEPS.index((dr, dc)), g * own4 : (g + 1) * own4, :]
                members.append(turn(piece, (dc + 1 - q) * QUARTER))
            at = PAD + (3 * k + dr + 1) * own4
            e4[0, at : at + own4, :] = beside(members)

    ext4 = 3 * own4
    ext5 = ext4 // 2
    shrink(e4, g5, "d4", STACK * ext5)
    coef3 = detail(3, g3, e4, u3, v3, "u3", rows3, ext4, 2 * (own4 - skip4), 0, rows3)
    coef4 = detail(4, e4, g5, u4, v4, "u4", ext4, ext5, 0, 0, ext4)

    guide_at = PAD + CHANNELS * ext5
    c5[0, PAD : PAD + ext5, :] = g5[0, guide_at : guide_at + ext5, :]

    def collapse(coarse, start, fine, at, coefficients, name):
        count = coefficients[0].shape[0] // 2
        for t in range(coarse.shape[0]):
            even, odd = row_up(coarse, t, PAD + start, count)
            u1[t, pl.ds(0, count, stride=2), :] = even
            u1[t, pl.ds(1, count, stride=2), :] = odd
        y = mm(wide([u1[t, 0 : 2 * count, :] for t in range(coarse.shape[0])]), matrix(name), 3)
        for t in range(fine.shape[0]):
            fine[t, PAD + at : PAD + at + 2 * count, :] = coefficients[t] + y[:, lane(t)]

    collapse(c5, 0, c4, 0, coef4, "u4")
    collapse(c4, own4 - skip4, c3, 0, coef3, "u3")
    collapse(c3, 0, c2, 0, coef2, "u2")
    collapse(c2, near // 2, c1, near, coef1, "u1")
    pairs = [row_up(c1, t, coarse_at, half) for t in range(tiles1)]
    x = jnp.concatenate([wide([p[0] for p in pairs]), wide([p[1] for p in pairs])], axis=0)
    fine = mm(x, matrix("u0"), 3)
    for t in range(own_tiles):
        for p in range(2):
            result[t, pl.ds(p, half, stride=2), :] = (
                gain[0] * total[t, p * half : (p + 1) * half, :]
                + fine[p * half : (p + 1) * half, lane(t)]
            )
        out[:, lane(t)] = result[t, :, :]


def tone(axes, luminance, level_gain):
    block_rows, block_cols = luminance.shape
    anchors = np.arange(CHANNELS, dtype=np.float32) / np.float32(CHANNELS - 1)
    down, up = matrices(block_cols)
    spans, parts, start = {}, [], 0
    width = max(m.shape[1] for m in down + up)
    for prefix, group in (("d", down), ("u", up)):
        for level, m in enumerate(group):
            spans[prefix + str(level)] = (start, *m.shape)
            parts.append(np.pad(m, ((0, 0), (0, width - m.shape[1]))))
            start += m.shape[0]
    bank = jnp.asarray(np.concatenate(parts), jnp.bfloat16)

    def f32(*shape):
        return pltpu.VMEM(shape, jnp.float32)

    def stack(tiles, count):
        return f32(tiles, ceil_to(count, 8) + 2 * PAD, LANE)

    own_tiles = block_cols // LANE
    tiles = [-(-len(circle(block_cols, l)) // LANE) for l in range(4)] + [1, 1]
    ext = block_rows + 2 * HALO
    rows = [ext >> l for l in range(5)]
    own4 = block_rows // 16
    ext4, ext5 = 3 * own4, 3 * own4 // 2
    side = block_rows // 4 + HALO // 2
    scratch = [
        f32(HALO, block_cols),
        f32(HALO, block_cols),
        f32(2, side, LANE),
        f32(2, side, LANE),
        f32(ext, LANE),
        f32(own_tiles, block_rows, LANE),
        stack(own_tiles + 1, ext),
        stack(tiles[1], rows[1]),
        f32(own_tiles, block_rows, LANE),
        f32(own_tiles, block_rows, LANE),
        pltpu.VMEM(bank.shape, jnp.bfloat16),
        stack(tiles[1], STACK * rows[1]),
        stack(tiles[2], STACK * rows[2]),
        stack(tiles[3], STACK * rows[3]),
        stack(1, STACK * rows[4]),
        stack(1, STACK * ext4),
        stack(1, STACK * ext5),
        stack(tiles[2], STACK * rows[1]),
        stack(tiles[3], STACK * rows[2]),
        stack(1, STACK * 2 * ext4),
        stack(1, STACK * ext4),
        stack(tiles[1], STACK * rows[1]),
        stack(tiles[2], STACK * rows[2]),
        stack(tiles[3], STACK * 2 * ext4),
        stack(1, STACK * ext4),
        stack(tiles[1], rows[1]),
        stack(tiles[2], rows[2]),
        stack(tiles[3], rows[3]),
        stack(1, ext4),
        stack(1, ext5),
        f32(-(-STACK // 4) * own4, LANE),
        f32(len(STEPS), -(-STACK // 4) * own4, LANE),
    ]
    dma = pltpu.SemaphoreType.DMA
    scratch += [dma((8,)), dma((8,)), dma((8,)), dma((8,)), dma]
    vmem = pl.BlockSpec(memory_space=pltpu.VMEM)
    smem = pl.BlockSpec(memory_space=pltpu.SMEM)
    return pl.pallas_call(
        functools.partial(kernel, axes, spans),
        out_shape=jax.ShapeDtypeStruct((block_rows, block_cols), jnp.float32),
        in_specs=[smem, smem, vmem, pl.BlockSpec(memory_space=pl.ANY)],
        out_specs=vmem,
        scratch_shapes=scratch,
        compiler_params=pltpu.CompilerParams(
            vmem_limit_bytes=48 * 1024 * 1024, collective_id=0, has_side_effects=True
        ),
        name="tone_pyramid",
    )(level_gain, jnp.asarray(anchors), luminance, bank)


def solution(mesh):
    placed = (P("row", "col"), P())

    def local(luminance, level_gain):
        return tone(("row", "col"), luminance, level_gain)

    return jax.shard_map(
        local, mesh=mesh, in_specs=placed, out_specs=P("row", "col"), check_vma=False
    )
```

time: 528 us -> 36.9 us (0.07)
  local copies, waits for them, and re-layouts: 353 us -> 4.7 us
  starting transfers between devices: 73.8 us -> 0 us
  other arithmetic: 58.1 us -> 0 us
  waiting for transfers between devices: 36.5 us -> 0 us
  Pallas kernels: 0 us -> 31.9 us
    slice x58 -> x0, local copies, waits for them, and re-layouts: 324 us -> none  [the longest x20 250 us: down_valid(): blurred[..., step:step + 2 * out_cols - 1:2]]
    ppermute x44 -> x0, starting transfers between devices: 73.8 us -> none  [the longest x22 63.5 us: with_halo(): lax.ppermute(lax.slice_in_dim(block, 0, width, axis=dim), axis, backward)]
    ppermute x44 -> x0, waiting for transfers between devices: 36.5 us -> none  [the longest x22 30.7 us: with_halo(): lax.ppermute(lax.slice_in_dim(block, block.shape[dim] - width, None, axis...]
    pallas_call x0 -> x1, Pallas kernels: none -> 31.9 us  [tone(): pl.pallas_call(functools.partial(kernel, axes, spans), out_shape=jax.Shap...]
    add x16 -> x0, other arithmetic: 22.2 us -> none  [the longest x5 8.19 us: down_valid(): result + binomial[step] * blurred[..., step:step + 2 * out_cols - 1:2]]
    another operation x38 -> x0, other arithmetic: 16.5 us -> none  [the longest x18 8.48 us: up_valid(): result = jnp.stack([even_cols, odd_cols], axis=-1)]
    another operation x17 -> x0, local copies, waits for them, and re-layouts: 13.1 us -> none  [the longest x8 12.3 us: up_valid(): result = jnp.stack([even_cols, odd_cols], axis=-1)]
    reshape x10 -> x0, local copies, waits for them, and re-layouts: 11.5 us -> none  [the longest x8 11.4 us: up_valid(): return result.reshape(result.shape[:-2] + (2 * (cols_in - 2),))]
  transfers between devices with their start and end apart: 44 -> 0, of which waited for: 21 -> 0; matrix products, arithmetic and copies ran while one was open for 9% -> 0% of each run, Pallas kernels for 0% -> 0%
where the time goes in v2:
time: 36.9 us; the launch traced here: 36.7 us
  Pallas kernels  31.9 us (86%)
  local copies, waits for them, and re-layouts  4.7 us (13%)
    pallas_call x1, Pallas kernels, tone(): pl.pallas_call(functools.partial(kernel, axes, spans), out_shape=jax.Shap...  31.9 us
    unnamed x9, local copies, waits for them, and re-layouts  4.7 us

profile of v2, /device:TPU:0, one launch (start us, length us, event | category | flops | bytes accessed | tf_op | source)
XLA Modules:
  0.0 36.7 jit_solution(5006583585575013002)
XLA Ops:
  0.0 0.0 copy-start
  0.0 1.7 %copy-done = bf16[2560,512]{1,0:T(8,128)(2,1)S(1)} copy-done((bf16[2560,512]{1,0:T(8,128)(2,1)S(1)}, bf16[2560,512]{1,0:T(8,128)(2,1)}, u32[]{:S(2)}) %copy-start) | copy-done | bytes 2621464
  1.7 0.0 copy-start.1
  1.7 0.9 %copy-done.1 = f32[128,512]{1,0:T(8,128)S(1)} copy-done((f32[128,512]{1,0:T(8,128)S(1)}, f32[128,512]{1,0:T(8,128)}, u32[]{:S(2)}) %copy-start.1) | copy-done | bytes 262168
  2.7 0.0 copy-start.2
  2.7 0.7 %copy-done.2 = f32[5]{0:T(128)S(1)} copy-done((f32[5]{0:T(128)S(1)}, f32[5]{0:T(128)}, u32[]{:S(2)}) %copy-start.2) | copy-done | bytes 44
  3.3 0.0 copy-start.3
  3.3 0.7 %copy-done.3 = f32[16]{0:T(128)S(1)} copy-done((f32[16]{0:T(128)S(1)}, f32[16]{0:T(128)}, u32[]{:S(2)}) %copy-start.3) | copy-done | bytes 88
  4.0 31.9 %tone_pyramid.1 = f32[128,512]{1,0:T(8,128)S(1)} custom-call(f32[5]{0:T(128)S(1)} %copy-done.2, f32[16]{0:T(128)S(1)} %copy-done.3, f32[128,512]{1,0:T(8,128)S(1)} %copy-done.1, bf16[2560,512]{1,0:T(8,128)(2,1)S(1)} %copy-done), custom_call_target="tpu_custom_call" | custom-call | tf_op jit(solution)/shard_map/tone_pyramid/pallas_call | solution.py:436
  36.0 0.7 %copy.6 = f32[128,512]{1,0:T(8,128)} copy(f32[128,512]{1,0:T(8,128)S(1)} %tone_pyramid.1) | data formatting | bytes 524288
Async XLA Ops:
  0.0 1.7 %copy-start = (bf16[2560,512]{1,0:T(8,128)(2,1)S(1)}, bf16[2560,512]{1,0:T(8,128)(2,1)}, u32[]{:S(2)}) copy-start(bf16[2560,512]{1,0:T(8,128)(2,1)} %constant.4.clone.bank) | copy-start | bytes 7864324
  1.7 0.9 %copy-start.1 = (f32[128,512]{1,0:T(8,128)S(1)}, f32[128,512]{1,0:T(8,128)}, u32[]{:S(2)}) copy-start(f32[128,512]{1,0:T(8,128)} %lum.1) | copy-start | bytes 786436
  2.7 0.7 %copy-start.2 = (f32[5]{0:T(128)S(1)}, f32[5]{0:T(128)}, u32[]{:S(2)}) copy-start(f32[5]{0:T(128)} %gain.1) | copy-start | bytes 64
  3.3 0.7 %copy-start.3 = (f32[16]{0:T(128)S(1)}, f32[16]{0:T(128)}, u32[]{:S(2)}) copy-start(f32[16]{0:T(128)} %constant.5.clone.anchors) | copy-start | bytes 196

commit v3 on v2

--- a/solution.py
+++ b/solution.py
@@ -11,6 +11,7 @@
 STACK = CHANNELS + 1
 HALO = 32
 PAD = 8
+GROUP = 4
 LANE = 128
 QUARTER = LANE // 4
 
@@ -71,13 +72,14 @@
 
 
 def mm(x, matrix, parts=2):
-    total = None
+    heads = []
     for part in range(parts):
-        head = x.astype(jnp.bfloat16)
+        heads.append(x.astype(jnp.bfloat16))
         if part < parts - 1:
-            x = x - head.astype(jnp.float32)
-        term = jnp.dot(head, matrix, preferred_element_type=jnp.float32)
-        total = term if total is None else total + term
+            x = x - heads[-1].astype(jnp.float32)
+    total = jnp.dot(wide(heads[:2]), matrix, preferred_element_type=jnp.float32)
+    if parts == 3:
+        total += jnp.dot(heads[2], matrix[: x.shape[1], :], preferred_element_type=jnp.float32)
     return total
 
 
@@ -90,6 +92,10 @@
     return jnp.maximum(0.0, 1.0 - jnp.abs(guidance - anchor) * (CHANNELS - 1))
 
 
+def anchor_of(k):
+    return np.float32(k) / np.float32(CHANNELS - 1)
+
+
 def wide(parts):
     return parts[0] if len(parts) == 1 else jnp.concatenate(parts, axis=1)
 
@@ -98,9 +104,11 @@
     return slice(t * LANE, (t + 1) * LANE)
 
 
-def row_down(ref, t, start, count):
+def row_down(ref, lead, start, count):
+    lead = lead if isinstance(lead, tuple) else (lead,)
+
     def tap(s):
-        return ref[t, pl.ds(start + s - 2, count, stride=2), :]
+        return ref[(*lead, pl.ds(start + s - 2, count, stride=2), slice(None))]
 
     return 0.375 * tap(2) + 0.25 * (tap(1) + tap(3)) + 0.0625 * (tap(0) + tap(4))
 
@@ -142,10 +150,10 @@
     return count
 
 
-def kernel(axes, spans, gain, anchors, lum, bank, out, *refs):
-    (top, bottom, side_out, side_in, halo, center, remapped, first, total, result, mats) = refs[:11]
-    (g1, g2, g3, g4, e4, g5, u1, u2, u3, u4, v1, v2, v3, v4, c1, c2, c3, c4, c5, packed, gathered) = refs[11:32]
-    send_a, recv_a, send_b, recv_b, bank_sem = refs[32:]
+def kernel(axes, spans, gain_hbm, lum_hbm, bank, out, *refs):
+    (gain, lum, top, bottom, side_out, side_in, halo, center, remapped, weights, first, total, result, mats) = refs[:14]
+    (g1, g2, g3, g4, e4, g5, u1, u2, u3, u4, v1, v2, v3, v4, c1, c2, c3, c4, c5, packed, gathered) = refs[14:35]
+    send_a, recv_a, send_b, recv_b, bank_sem, lum_sem, gain_sem = refs[35:]
     block_rows, block_cols = lum.shape
     own_tiles = block_cols // LANE
     half = block_rows // 2
@@ -156,23 +164,26 @@
         return tuple(lax.rem(p + d + n, n) for p, d, n in zip(place, (dr, dc), counts))
 
     def matrix(name):
-        start, depth, width = spans[name]
-        return mats[start : start + depth, 0:width]
-
-    bank_copy = pltpu.make_async_copy(bank, mats, bank_sem)
-    bank_copy.start()
+        start, depth, count = spans[name]
+        whole = wide([mats[start + t * depth : start + (t + 1) * depth, :] for t in range(count)])
+        return jnp.concatenate([whole, whole], axis=0)
+
     barrier = pltpu.get_barrier_semaphore()
     for dr, dc in STEPS:
         pl.semaphore_signal(barrier, inc=1, device_id=device(dr, dc), device_id_type=MESH)
+    lum_copy = pltpu.make_async_copy(lum_hbm, lum, lum_sem)
+    lum_copy.start()
+    gain_copy = pltpu.make_async_copy(gain_hbm, gain, gain_sem)
+    gain_copy.start()
+    bank_copy = pltpu.make_async_copy(bank, mats, bank_sem)
+    bank_copy.start()
+    lum_copy.wait()
 
     mid, corner = block_rows // 4, HALO // 4
     for s, (t, start) in enumerate(((0, 0), (own_tiles - 1, LANE - QUARTER))):
         side_out[s, 0:mid, :] = pack(lum[:, lane(t)], start)
         side_out[s, mid : mid + corner, :] = pack(lum[0:HALO, lane(t)], start)
         side_out[s, mid + corner : mid + 2 * corner, :] = pack(lum[block_rows - HALO :, lane(t)], start)
-    for t in range(own_tiles):
-        center[t, :, :] = lum[:, lane(t)]
-    total[...] = jnp.zeros_like(total)
     pl.semaphore_wait(barrier, len(STEPS))
 
     rows_at = {0: (0, mid), -1: (mid, corner), 1: (mid + corner, corner)}
@@ -195,9 +206,28 @@
         )
         copy.start()
         copies.append(copy)
+    for t in range(own_tiles):
+        center[t, :, :] = lum[:, lane(t)]
+    total[...] = jnp.zeros_like(total)
+
+    def own_cells(t, carry):
+        for r in range(0, block_rows, 32):
+            values = center[t, r : r + 32, :]
+            remapped[CHANNELS, t, PAD + HALO + r : PAD + HALO + r + 32, :] = values
+            running = 0.5 * values
+            for k in range(CHANNELS):
+                value, weight = bump(values, anchor_of(k)), hat(values, anchor_of(k))
+                remapped[k, t, PAD + HALO + r : PAD + HALO + r + 32, :] = value
+                weights[k, t, r : r + 32, :] = weight
+                running = running + weight * value
+            result[t, r : r + 32, :] = running
+        return carry
+
+    lax.fori_loop(0, own_tiles, own_cells, 0)
     for copy in copies:
         copy.wait()
     bank_copy.wait()
+    gain_copy.wait()
 
     ext_rows = block_rows + 2 * HALO
     for start, (at, count) in ((0, rows_at[-1]), (HALO, rows_at[0]), (HALO + block_rows, rows_at[1])):
@@ -208,46 +238,53 @@
                 index < LANE // 2, turn(right, -g * QUARTER), turn(left, LANE - QUARTER - g * QUARTER)
             )
 
-    def extended(t):
+    def beyond(t):
         if t == own_tiles:
             return [(r, halo[r : r + 64, :]) for r in range(0, ext_rows, 64)]
-        inner = [(HALO + r, lum[r : r + 64, lane(t)]) for r in range(0, block_rows, 64)]
-        return [(0, top[:, lane(t)])] + inner + [(HALO + block_rows, bottom[:, lane(t)])]
+        return [(0, top[:, lane(t)]), (HALO + block_rows, bottom[:, lane(t)])]
 
     rows1 = ext_rows // 2
     tiles1 = first.shape[0]
     coarse_at = PAD + HALO // 2
 
-    def finest(dst_row, prepare, weigh):
-        for t in range(own_tiles + 1):
-            for r, values in extended(t):
-                remapped[t, PAD + r : PAD + r + values.shape[0], :] = prepare(values)
-        x = wide([row_down(remapped, t, PAD, rows1) for t in range(own_tiles + 1)])
-        y = mm(x, matrix("d0"))
+    def finest(members, dst_row, prepare, weigh):
+        for k in members:
+            for t in range(own_tiles + 1):
+                for r, values in beyond(t):
+                    remapped[k, t, PAD + r : PAD + r + values.shape[0], :] = prepare(values, k)
+        x = [
+            wide([row_down(remapped, (k, t), PAD, rows1) for t in range(own_tiles + 1)])
+            for k in members
+        ]
+        y = mm(jnp.concatenate(x, axis=0), matrix("d0"))
+        count = len(members) * rows1
         for t in range(tiles1):
-            g1[t, pl.ds(dst_row, rows1), :] = y[:, lane(t)]
-            first[t, PAD : PAD + rows1, :] = y[:, lane(t)]
-        pairs = [row_up(first, t, coarse_at, half) for t in range(tiles1)]
-        x = jnp.concatenate([wide([p[0] for p in pairs]), wide([p[1] for p in pairs])], axis=0)
-        fine = mm(x, matrix("u0"))
+            g1[t, pl.ds(dst_row, count), :] = y[:, lane(t)]
+            first[t, PAD : PAD + count, :] = y[:, lane(t)]
+        x = []
+        for q in range(len(members)):
+            pairs = [row_up(first, t, coarse_at + q * rows1, half) for t in range(tiles1)]
+            x += [wide([p[0] for p in pairs]), wide([p[1] for p in pairs])]
+        fine = mm(jnp.concatenate(x, axis=0), matrix("u0"))
         for t in range(own_tiles):
             for p in range(2):
-                value = remapped[t, pl.ds(PAD + HALO + p, half, stride=2), :]
-                total[t, p * half : (p + 1) * half, :] += weigh(t, p) * (
-                    value - fine[p * half : (p + 1) * half, lane(t)]
-                )
-
-    def channel(k, carry):
-        anchor = anchors[k]
+                running = total[t, p * half : (p + 1) * half, :]
+                for q, k in enumerate(members):
+                    at = (2 * q + p) * half
+                    running = running + weigh(k, t, p) * fine[at : at + half, lane(t)]
+                total[t, p * half : (p + 1) * half, :] = running
+
+    def channels(j, carry):
         finest(
-            pl.multiple_of(PAD + k * rows1, 8),
-            lambda values: bump(values, anchor),
-            lambda t, p: hat(center[t, pl.ds(p, half, stride=2), :], anchor),
+            [GROUP * j + q for q in range(GROUP)],
+            pl.multiple_of(PAD + GROUP * j * rows1, 8),
+            lambda values, k: bump(values, k.astype(jnp.float32) * np.float32(1.0 / (CHANNELS - 1))),
+            lambda k, t, p: weights[k, t, pl.ds(p, half, stride=2), :],
         )
         return carry
 
-    lax.fori_loop(0, CHANNELS, channel, 0)
-    finest(PAD + CHANNELS * rows1, lambda values: values, lambda t, p: 0.5)
+    lax.fori_loop(0, CHANNELS // GROUP, channels, 0)
+    finest([CHANNELS], PAD + CHANNELS * rows1, lambda values, k: values, lambda k, t, p: 0.5)
 
     def shrink(src, dst, name, count):
         step = chunk_of(count)
@@ -310,8 +347,7 @@
             guidance = fine_stack[t, PAD + CHANNELS * fine + a : PAD + CHANNELS * fine + b, :]
             running = 0.5 * difference(CHANNELS)
             for k in range(CHANNELS):
-                anchor = np.float32(k) / np.float32(CHANNELS - 1)
-                running = running + hat(guidance, anchor) * difference(k)
+                running = running + hat(guidance, anchor_of(k)) * difference(k)
             sums.append(gain[level] * running)
         return sums
 
@@ -362,24 +398,23 @@
     fine = mm(x, matrix("u0"), 3)
     for t in range(own_tiles):
         for p in range(2):
+            own = result[t, pl.ds(p, half, stride=2), :] - total[t, p * half : (p + 1) * half, :]
             result[t, pl.ds(p, half, stride=2), :] = (
-                gain[0] * total[t, p * half : (p + 1) * half, :]
-                + fine[p * half : (p + 1) * half, lane(t)]
+                gain[0] * own + fine[p * half : (p + 1) * half, lane(t)]
             )
         out[:, lane(t)] = result[t, :, :]
 
 
 def tone(axes, luminance, level_gain):
     block_rows, block_cols = luminance.shape
-    anchors = np.arange(CHANNELS, dtype=np.float32) / np.float32(CHANNELS - 1)
     down, up = matrices(block_cols)
     spans, parts, start = {}, [], 0
-    width = max(m.shape[1] for m in down + up)
     for prefix, group in (("d", down), ("u", up)):
         for level, m in enumerate(group):
-            spans[prefix + str(level)] = (start, *m.shape)
-            parts.append(np.pad(m, ((0, 0), (0, width - m.shape[1]))))
-            start += m.shape[0]
+            count = m.shape[1] // LANE
+            spans[prefix + str(level)] = (start, m.shape[0], count)
+            parts += [m[:, lane(t)] for t in range(count)]
+            start += m.shape[0] * count
     bank = jnp.asarray(np.concatenate(parts), jnp.bfloat16)
 
     def f32(*shape):
@@ -396,14 +431,17 @@
     ext4, ext5 = 3 * own4, 3 * own4 // 2
     side = block_rows // 4 + HALO // 2
     scratch = [
+        pltpu.SMEM(level_gain.shape, jnp.float32),
+        f32(block_rows, block_cols),
         f32(HALO, block_cols),
         f32(HALO, block_cols),
         f32(2, side, LANE),
         f32(2, side, LANE),
         f32(ext, LANE),
         f32(own_tiles, block_rows, LANE),
-        stack(own_tiles + 1, ext),
-        stack(tiles[1], rows[1]),
+        f32(STACK, own_tiles + 1, ext + 2 * PAD, LANE),
+        f32(CHANNELS, own_tiles, block_rows, LANE),
+        stack(tiles[1], GROUP * rows[1]),
         f32(own_tiles, block_rows, LANE),
         f32(own_tiles, block_rows, LANE),
         pltpu.VMEM(bank.shape, jnp.bfloat16),
@@ -430,20 +468,20 @@
         f32(len(STEPS), -(-STACK // 4) * own4, LANE),
     ]
     dma = pltpu.SemaphoreType.DMA
-    scratch += [dma((8,)), dma((8,)), dma((8,)), dma((8,)), dma]
+    scratch += [dma((8,)), dma((8,)), dma((8,)), dma((8,)), dma, dma, dma]
     vmem = pl.BlockSpec(memory_space=pltpu.VMEM)
-    smem = pl.BlockSpec(memory_space=pltpu.SMEM)
+    hbm = pl.BlockSpec(memory_space=pltpu.HBM)
     return pl.pallas_call(
         functools.partial(kernel, axes, spans),
         out_shape=jax.ShapeDtypeStruct((block_rows, block_cols), jnp.float32),
-        in_specs=[smem, smem, vmem, pl.BlockSpec(memory_space=pl.ANY)],
+        in_specs=[hbm, hbm, hbm],
         out_specs=vmem,
         scratch_shapes=scratch,
         compiler_params=pltpu.CompilerParams(
-            vmem_limit_bytes=48 * 1024 * 1024, collective_id=0, has_side_effects=True
+            vmem_limit_bytes=56 * 1024 * 1024, collective_id=0, has_side_effects=True
         ),
         name="tone_pyramid",
-    )(level_gain, jnp.asarray(anchors), luminance, bank)
+    )(level_gain, luminance, bank)
 
 
 def solution(mesh):

time: 36.9 us -> 27.3 us (0.74)
  Pallas kernels: 31.9 us -> 25.4 us
  local copies, waits for them, and re-layouts: 4.7 us -> 1.67 us
    pallas_call x1, Pallas kernels: 31.9 us -> 25.4 us  [tone(): pl.pallas_call(functools.partial(kernel, axes, spans), out_shape=jax.Shap...]
    unnamed x9 -> x1, local copies, waits for them, and re-layouts: 4.7 us -> 1.67 us
where the time goes in v3:
time: 27.3 us; the launch traced here: 27.1 us
  Pallas kernels  25.4 us (93%)
  local copies, waits for them, and re-layouts  1.67 us (6%)
    pallas_call x1, Pallas kernels, tone(): pl.pallas_call(functools.partial(kernel, axes, spans), out_shape=jax.Shap...  25.4 us
    unnamed x1, local copies, waits for them, and re-layouts  1.67 us

profile of v3, /device:TPU:0, one launch (start us, length us, event | category | flops | bytes accessed | tf_op | source)
XLA Modules:
  0.0 27.1 jit_solution(3412413949684508588)
XLA Ops:
  0.0 25.4 %tone_pyramid.1 = f32[128,512]{1,0:T(8,128)} custom-call(f32[5]{0:T(128)} %gain_hbm.1, f32[128,512]{1,0:T(8,128)} %lum_hbm.1, bf16[6016,128]{1,0:T(8,128)(2,1)} %constant.2.clone.bank), custom_call_target="tpu_custom_call" | custom-call | tf_op jit(solution)/shard_map/tone_pyramid/pallas_call | solution.py:474
  25.4 1.7 %copy.5 = f32[128,512]{1,0:T(8,128)} copy(f32[128,512]{1,0:T(8,128)} %tone_pyramid.1) | data formatting | bytes 524288

commit v4 on v3

--- a/solution.py
+++ b/solution.py
@@ -11,7 +11,7 @@
 STACK = CHANNELS + 1
 HALO = 32
 PAD = 8
-GROUP = 4
+GROUP = 8
 LANE = 128
 QUARTER = LANE // 4
 
@@ -151,9 +151,9 @@
 
 
 def kernel(axes, spans, gain_hbm, lum_hbm, bank, out, *refs):
-    (gain, lum, top, bottom, side_out, side_in, halo, center, remapped, weights, first, total, result, mats) = refs[:14]
-    (g1, g2, g3, g4, e4, g5, u1, u2, u3, u4, v1, v2, v3, v4, c1, c2, c3, c4, c5, packed, gathered) = refs[14:35]
-    send_a, recv_a, send_b, recv_b, bank_sem, lum_sem, gain_sem = refs[35:]
+    (gain, lum, top, bottom, side_out, side_in, halo, center, remapped, weights, total, result, mats) = refs[:13]
+    (g1, g2, g3, g4, e4, g5, u1, u2, u3, u4, v1, v2, v3, v4, c1, c2, c3, c4, c5, packed, gathered) = refs[13:34]
+    send_a, recv_a, send_b, recv_b, bank_sem, lum_sem, gain_sem = refs[34:]
     block_rows, block_cols = lum.shape
     own_tiles = block_cols // LANE
     half = block_rows // 2
@@ -244,10 +244,10 @@
         return [(0, top[:, lane(t)]), (HALO + block_rows, bottom[:, lane(t)])]
 
     rows1 = ext_rows // 2
-    tiles1 = first.shape[0]
+    tiles1 = g1.shape[0]
     coarse_at = PAD + HALO // 2
 
-    def finest(members, dst_row, prepare, weigh):
+    def finest_down(members, dst_row, prepare):
         for k in members:
             for t in range(own_tiles + 1):
                 for r, values in beyond(t):
@@ -257,13 +257,24 @@
             for k in members
         ]
         y = mm(jnp.concatenate(x, axis=0), matrix("d0"))
-        count = len(members) * rows1
         for t in range(tiles1):
-            g1[t, pl.ds(dst_row, count), :] = y[:, lane(t)]
-            first[t, PAD : PAD + count, :] = y[:, lane(t)]
+            g1[t, pl.ds(dst_row, len(members) * rows1), :] = y[:, lane(t)]
+
+    def channels(j, carry):
+        finest_down(
+            [GROUP * j + q for q in range(GROUP)],
+            pl.multiple_of(PAD + GROUP * j * rows1, 8),
+            lambda values, k: bump(values, k.astype(jnp.float32) * np.float32(1.0 / (CHANNELS - 1))),
+        )
+        return carry
+
+    lax.fori_loop(0, CHANNELS // GROUP, channels, 0)
+    finest_down([CHANNELS], PAD + CHANNELS * rows1, lambda values, k: values)
+
+    def finest_up(members):
         x = []
-        for q in range(len(members)):
-            pairs = [row_up(first, t, coarse_at + q * rows1, half) for t in range(tiles1)]
+        for k in members:
+            pairs = [row_up(g1, t, coarse_at + k * rows1, half) for t in range(tiles1)]
             x += [wide([p[0] for p in pairs]), wide([p[1] for p in pairs])]
         fine = mm(jnp.concatenate(x, axis=0), matrix("u0"))
         for t in range(own_tiles):
@@ -271,20 +282,9 @@
                 running = total[t, p * half : (p + 1) * half, :]
                 for q, k in enumerate(members):
                     at = (2 * q + p) * half
-                    running = running + weigh(k, t, p) * fine[at : at + half, lane(t)]
+                    weight = 0.5 if k == CHANNELS else weights[k, t, pl.ds(p, half, stride=2), :]
+                    running = running + weight * fine[at : at + half, lane(t)]
                 total[t, p * half : (p + 1) * half, :] = running
-
-    def channels(j, carry):
-        finest(
-            [GROUP * j + q for q in range(GROUP)],
-            pl.multiple_of(PAD + GROUP * j * rows1, 8),
-            lambda values, k: bump(values, k.astype(jnp.float32) * np.float32(1.0 / (CHANNELS - 1))),
-            lambda k, t, p: weights[k, t, pl.ds(p, half, stride=2), :],
-        )
-        return carry
-
-    lax.fori_loop(0, CHANNELS // GROUP, channels, 0)
-    finest([CHANNELS], PAD + CHANNELS * rows1, lambda values, k: values, lambda k, t, p: 0.5)
 
     def shrink(src, dst, name, count):
         step = chunk_of(count)
@@ -351,6 +351,8 @@
             sums.append(gain[level] * running)
         return sums
 
+    for k in range(0, CHANNELS, 4):
+        finest_up(list(range(k, STACK if k + 4 == CHANNELS else k + 4)))
     near = HALO // 2 - 8
     coef1 = detail(1, g1, g2, u1, v1, "u1", rows1, rows2, 0, near, rows1 - near)
     coef2 = detail(2, g2, g3, u2, v2, "u2", rows2, rows3, 0, 0, rows2)
@@ -441,7 +443,6 @@
         f32(own_tiles, block_rows, LANE),
         f32(STACK, own_tiles + 1, ext + 2 * PAD, LANE),
         f32(CHANNELS, own_tiles, block_rows, LANE),
-        stack(tiles[1], GROUP * rows[1]),
         f32(own_tiles, block_rows, LANE),
         f32(own_tiles, block_rows, LANE),
         pltpu.VMEM(bank.shape, jnp.bfloat16),

time: 27.3 us -> 24.6 us (0.901)
  Pallas kernels: 25.4 us -> 22.7 us
    pallas_call x1, Pallas kernels: 25.4 us -> 22.7 us  [tone(): pl.pallas_call(functools.partial(kernel, axes, spans), out_shape=jax.Shap...]
where the time goes in v4:
time: 24.6 us; the launch traced here: 24.4 us
  Pallas kernels  22.7 us (92%)
  local copies, waits for them, and re-layouts  1.67 us (7%)
    pallas_call x1, Pallas kernels, tone(): pl.pallas_call(functools.partial(kernel, axes, spans), out_shape=jax.Shap...  22.7 us
    unnamed x1, local copies, waits for them, and re-layouts  1.67 us

profile of v4, /device:TPU:0, one launch (start us, length us, event | category | flops | bytes accessed | tf_op | source)
XLA Modules:
  0.0 24.4 jit_solution(9237165016787468358)
XLA Ops:
  0.0 22.7 %tone_pyramid.1 = f32[128,512]{1,0:T(8,128)} custom-call(f32[5]{0:T(128)} %gain_hbm.1, f32[128,512]{1,0:T(8,128)} %lum_hbm.1, bf16[6016,128]{1,0:T(8,128)(2,1)} %constant.2.clone.bank), custom_call_target="tpu_custom_call" | custom-call | tf_op jit(solution)/shard_map/tone_pyramid/pallas_call | solution.py:475
  22.8 1.7 %copy.5 = f32[128,512]{1,0:T(8,128)} copy(f32[128,512]{1,0:T(8,128)} %tone_pyramid.1) | data formatting | bytes 524288

commit v5 on v4

--- a/solution.py
+++ b/solution.py
@@ -260,16 +260,11 @@
         for t in range(tiles1):
             g1[t, pl.ds(dst_row, len(members) * rows1), :] = y[:, lane(t)]
 
-    def channels(j, carry):
-        finest_down(
-            [GROUP * j + q for q in range(GROUP)],
-            pl.multiple_of(PAD + GROUP * j * rows1, 8),
-            lambda values, k: bump(values, k.astype(jnp.float32) * np.float32(1.0 / (CHANNELS - 1))),
-        )
-        return carry
-
-    lax.fori_loop(0, CHANNELS // GROUP, channels, 0)
-    finest_down([CHANNELS], PAD + CHANNELS * rows1, lambda values, k: values)
+    def prepared(values, k):
+        return values if k == CHANNELS else bump(values, anchor_of(k))
+
+    finest_down(list(range(GROUP)), PAD, prepared)
+    finest_down(list(range(GROUP, STACK)), PAD + GROUP * rows1, prepared)
 
     def finest_up(members):
         x = []

time: 24.6 us -> 24.1 us (0.980)
  Pallas kernels: 22.7 us -> 22.3 us
    pallas_call x1, Pallas kernels: 22.7 us -> 22.3 us  [tone(): pl.pallas_call(functools.partial(kernel, axes, spans), out_shape=jax.Shap...]
where the time goes in v5:
time: 24.1 us; the launch traced here: 24 us
  Pallas kernels  22.3 us (93%)
  local copies, waits for them, and re-layouts  1.67 us (7%)
    pallas_call x1, Pallas kernels, tone(): pl.pallas_call(functools.partial(kernel, axes, spans), out_shape=jax.Shap...  22.3 us
    unnamed x1, local copies, waits for them, and re-layouts  1.67 us

profile of v5, /device:TPU:0, one launch (start us, length us, event | category | flops | bytes accessed | tf_op | source)
XLA Modules:
  0.0 24.0 jit_solution(1942910605188720961)
XLA Ops:
  0.0 22.3 %tone_pyramid.1 = f32[128,512]{1,0:T(8,128)} custom-call(f32[5]{0:T(128)} %gain_hbm.1, f32[128,512]{1,0:T(8,128)} %lum_hbm.1, bf16[6016,128]{1,0:T(8,128)(2,1)} %constant.2.clone.bank), custom_call_target="tpu_custom_call" | custom-call | tf_op jit(solution)/shard_map/tone_pyramid/pallas_call | solution.py:470
  22.3 1.7 %copy.5 = f32[128,512]{1,0:T(8,128)} copy(f32[128,512]{1,0:T(8,128)} %tone_pyramid.1) | data formatting | bytes 524288
